TPU v7x, 32 devices: a whole 2x2x4 slice. The times are simulated.
32 devices in a mesh: dp: 16 (over z, y, core), fsdp: 2 (over x).
Axes of the slice: x: 2, y: 2, z: 4, core: 2. Of those that a mesh axis runs over, the one named last changes fastest.
Arguments:
- captions: bfloat16 [32, 128, 768], P(('dp', 'fsdp')), may hold values from -6 to 6
- tiles: bfloat16 [32, 196, 768], P(('dp', 'fsdp')), may hold values from -6 to 6
- tile_index: int32 [32, 4], P(('dp', 'fsdp')), may hold values from 0 to 1
- tile_valid: int32 [32, 4], P(('dp', 'fsdp')), may hold values from 0 to 1
- caption_len: int32 [32], P(('dp', 'fsdp')), may hold values from 32 to 128
- weights: bfloat16 [73984, 128], P('fsdp')
- first_moment: float32 [73984, 128], P(('dp', 'fsdp')), may hold values from -0.00024414062 to 0.00024414062
- second_moment: float32 [73984, 128], P(('dp', 'fsdp')), may hold values from 2e-11 to 5e-10
- d_out: bfloat16 [32, 128, 768], P(('dp', 'fsdp')), may hold values from -6 to 6
Outputs:
- output: bfloat16 [32, 128, 768], P(('dp', 'fsdp'))
- d_captions: float32 [32, 128, 768], P(('dp', 'fsdp'))
- d_tiles: float32 [32, 196, 768], P(('dp', 'fsdp'))
- grads: float32 [73984, 128], P(('dp', 'fsdp'))
- update: float32 [73984, 128], P(('dp', 'fsdp'))
- new_first: float32 [73984, 128], P(('dp', 'fsdp'))
- new_second: float32 [73984, 128], P(('dp', 'fsdp'))
- grad_norm: float32 [], replicated
- tensor_rms: float32 [21], replicated
Inputs may be any that keep to these rules, and one draw needn't show every extreme that they name: `tile_index`: indices count the tiles of the caption's own dp index.
All inputs are finite; a program needn't handle non-finite values.
Results may differ from a plain program's by a relative error of at most 0.018.
Values may be sent and summed in bfloat16 or wider, within the bound.
A program may use at most 256 MiB of HBM per device.

v0:
```python
import jax
import jax.numpy as jnp
import numpy as np
from jax import lax
from jax.experimental import pallas as pl
from jax.experimental.pallas import tpu as pltpu
from jax.sharding import PartitionSpec as P

HEADS = 12
HEAD_DIM = 64
FF = 3072
STEP = 10


EPS_NORM = 1e-05
CLIP_NORM = 1.0
BETA_ONE = 0.9
BETA_TWO = 0.999
LEARN_RATE = 0.01
DECAY_RATE = 0.1
ADAM_EPS = 1e-08
NEG_LARGE = -1e30
(NORM_ONE_GAIN, NORM_ONE_SHIFT, SELF_QKV, SELF_QUERY_BIAS, SELF_VALUE_BIAS, SELF_OUT, SELF_OUT_BIAS, NORM_TWO_GAIN, NORM_TWO_SHIFT, CROSS_QUERY, CROSS_QUERY_BIAS, CROSS_KV, CROSS_VALUE_BIAS, CROSS_OUT, CROSS_OUT_BIAS, NORM_THREE_GAIN, NORM_THREE_SHIFT, MLP_UP, MLP_UP_BIAS, MLP_DOWN, MLP_DOWN_BIAS) = range(21)
DP, FSDP = "dp", "fsdp"
BOTH = (DP, FSDP)
E_BHQK_BKHE_TO_BQHE = "bhqk,bkhe->bqhe"
E_BHQK_BQHE_TO_BKHE = "bhqk,bqhe->bkhe"
E_BLD_BLE_TO_DE = "bld,ble->de"
E_BLD_BLF_TO_DF = "bld,blf->df"
E_BLD_DE_TO_BLE = "bld,de->ble"
E_BLD_DF_TO_BLF = "bld,df->blf"
E_BLD_FD_TO_BLF = "bld,fd->blf"
E_BLE_DE_TO_BLD = "ble,de->bld"
E_BLF_BLD_TO_FD = "blf,bld->fd"
E_BLF_DF_TO_BLD = "blf,df->bld"
E_BLF_FD_TO_BLD = "blf,fd->bld"
E_BQHE_BKHE_TO_BHQK = "bqhe,bkhe->bhqk"
E_CSG_CSPE_TO_GPE = "csg,cspe->gpe"
E_TPD_DE_TO_TPE = "tpd,de->tpe"
E_TPD_TPE_TO_DE = "tpd,tpe->de"
E_TPE_DE_TO_TPD = "tpe,de->tpd"


def for_sending(x):
    return jax.tree.map(lambda a: a.astype(jnp.bfloat16) if a.dtype == jnp.float32 else a, x)


def layout(model_width, hidden_width):
    return [
        (NORM_ONE_GAIN, (model_width,), 0),
        (NORM_ONE_SHIFT, (model_width,), 0),
        (SELF_QKV, (model_width, 3 * model_width), 1),
        (SELF_QUERY_BIAS, (model_width,), 0),
        (SELF_VALUE_BIAS, (model_width,), 0),
        (SELF_OUT, (model_width, model_width), 1),
        (SELF_OUT_BIAS, (model_width,), 0),
        (NORM_TWO_GAIN, (model_width,), 0),
        (NORM_TWO_SHIFT, (model_width,), 0),
        (CROSS_QUERY, (model_width, model_width), 1),
        (CROSS_QUERY_BIAS, (model_width,), 0),
        (CROSS_KV, (model_width, 2 * model_width), 1),
        (CROSS_VALUE_BIAS, (model_width,), 0),
        (CROSS_OUT, (model_width, model_width), 1),
        (CROSS_OUT_BIAS, (model_width,), 0),
        (NORM_THREE_GAIN, (model_width,), 0),
        (NORM_THREE_SHIFT, (model_width,), 0),
        (MLP_UP, (model_width, hidden_width), 1),
        (MLP_UP_BIAS, (hidden_width,), 0),
        (MLP_DOWN, (hidden_width, model_width), 1),
        (MLP_DOWN_BIAS, (model_width,), 0),
    ]


def segment_table(model_width, hidden_width):
    seg_starts = []
    seg_ends = []
    decay_flags = []
    seg_entries = []
    row_at = 0
    for seg_label, seg_shape, seg_flag in layout(model_width, hidden_width):
        item_count = int(np.prod(seg_shape))
        seg_rows = item_count // 128
        seg_starts.append(row_at)
        seg_ends.append(row_at + seg_rows)
        decay_flags.append(seg_flag == 1)
        seg_entries.append(float(item_count))
        row_at = row_at + seg_rows
    return (np.array(seg_starts), np.array(seg_ends), np.array(decay_flags), np.array(seg_entries))


def unpack(flat_rows, model_width, hidden_width):
    vector = flat_rows.reshape(-1)
    tensors = {}
    offset = 0
    for seg_label, seg_shape, seg_flag in layout(model_width, hidden_width):
        item_count = int(np.prod(seg_shape))
        tensors[seg_label] = vector[offset : offset + item_count].reshape(seg_shape)
        offset = offset + item_count
    return tensors


def pack_rows(gradients, model_width, hidden_width, total_rows):
    pieces = [
        gradients[seg_label].reshape(-1, 128)
        for seg_label, seg_shape, seg_flag in layout(model_width, hidden_width)
    ]
    used_rows = sum((tensor_piece.shape[0] for tensor_piece in pieces))
    pieces.append(jnp.zeros((total_rows - used_rows, 128), jnp.float32))
    return jnp.concatenate(pieces, axis=0)


def product(pattern, left_side, right_side):
    return jnp.einsum(pattern, left_side, right_side, preferred_element_type=jnp.float32)


def as_float(tensors, seg_label):
    return tensors[seg_label].astype(jnp.float32)


def column_sums(values):
    return jnp.sum(values.astype(jnp.float32), axis=tuple(range(values.ndim - 1)))


def layer_norm(values, gain_term, offset_term):
    center = values - jnp.mean(values, axis=-1, keepdims=True)
    spread = jnp.mean(center * center, axis=-1, keepdims=True)
    return center * lax.rsqrt(spread + EPS_NORM) * gain_term + offset_term


def gelu_exact(pre_values):
    return jax.nn.gelu(pre_values, approximate=False)


def norm_back(values, tensors, gain, shift, normed_grad, gradients):
    norm_value, norm_pull = jax.vjp(
        layer_norm,
        values,
        as_float(tensors, gain),
        as_float(tensors, shift),
    )
    values_grad, gain_grad, offset_grad = norm_pull(normed_grad)
    gradients[gain] = gain_grad
    gradients[shift] = offset_grad
    return values_grad


def score_block(queries, key_head_split, allowed):
    scores = product(E_BQHE_BKHE_TO_BHQK, queries, key_head_split) * 0.125
    return jnp.where(allowed, scores, NEG_LARGE)


def softmax_forward(queries, key_head_split, allowed):
    scores = score_block(queries, key_head_split, allowed)
    highest = jnp.max(scores, axis=-1, keepdims=True)
    exponent = jnp.exp(scores - highest)
    row_total = jnp.sum(exponent, axis=-1, keepdims=True)
    return (exponent / row_total, highest + jnp.log(row_total))


def attention_backward_pass(queries, key_head_split, values, allowed, log_total, mixed_grad):
    probabilities = jnp.where(
        allowed, jnp.exp(score_block(queries, key_head_split, allowed) - log_total), 0.0
    )
    probs_grad = product(E_BQHE_BKHE_TO_BHQK, mixed_grad, values)
    values_grad = product(E_BHQK_BQHE_TO_BKHE, probabilities.astype(jnp.bfloat16), mixed_grad)
    inner_sum = jnp.sum(probabilities * probs_grad, axis=-1, keepdims=True)
    score_grad = (probabilities * (probs_grad - inner_sum)).astype(jnp.bfloat16)
    queries_grad = product(E_BHQK_BKHE_TO_BQHE, score_grad, key_head_split) * 0.125
    keys_grad = product(E_BHQK_BQHE_TO_BKHE, score_grad, queries) * 0.125
    return (queries_grad, keys_grad, values_grad)


def adam_step(
    gradients,
    member,
    decay_flags,
    old_weights,
    first_moment,
    second_moment,
    square_sums,
    seg_entries,
):
    grad_norm = jnp.sqrt(jnp.sum(square_sums))
    tensor_rms = jnp.sqrt(square_sums / jnp.asarray(seg_entries, dtype=square_sums.dtype))
    clip_scale = jnp.minimum(1.0, CLIP_NORM / (grad_norm + 1e-06))
    clipped = gradients * clip_scale
    new_first = BETA_ONE * first_moment + (1.0 - BETA_ONE) * clipped
    new_second = BETA_TWO * second_moment + (1.0 - BETA_TWO) * clipped * clipped
    first_hat = new_first / (1.0 - BETA_ONE**STEP)
    second_hat = new_second / (1.0 - BETA_TWO**STEP)
    decay_rows = jnp.any(member & decay_flags[None, :], axis=1)
    decayed = jnp.where(decay_rows[:, None], old_weights, 0.0)
    update = -LEARN_RATE * (first_hat / (jnp.sqrt(second_hat) + ADAM_EPS) + DECAY_RATE * decayed)
    return (update, new_first, new_second, grad_norm, tensor_rms)


def body(
    captions,
    tiles,
    tile_index,
    tile_valid,
    caption_len,
    weights,
    first_moment,
    second_moment,
    d_out,
):
    model_width = captions.shape[2]
    hidden_width = FF
    caption_rows = captions.shape[0]
    cap_length = captions.shape[1]
    patch_count = tiles.shape[1]
    own_tiles = tiles.shape[0]
    slot_count = tile_index.shape[1]
    group_size = lax.axis_size(FSDP)
    data_size = lax.axis_size(DP)
    total_rows = weights.shape[0] * group_size
    heads_shape = (caption_rows, cap_length, HEADS, HEAD_DIM)
    key_shape = (caption_rows, slot_count * patch_count, HEADS, HEAD_DIM)
    token_layout_form = (caption_rows, cap_length, model_width)
    tensors = unpack(lax.all_gather(weights, FSDP, axis=0, tiled=True), model_width, hidden_width)
    zero_part = jnp.zeros((model_width,), jnp.bfloat16)
    input_values = captions.astype(jnp.float32)
    normed_one = layer_norm(
        input_values, as_float(tensors, NORM_ONE_GAIN), as_float(tensors, NORM_ONE_SHIFT)
    ).astype(jnp.bfloat16)
    qkv_bias = jnp.concatenate(
        [tensors[SELF_QUERY_BIAS], zero_part, tensors[SELF_VALUE_BIAS]]
    ).astype(jnp.float32)
    packed_qkv = (product(E_BLD_DE_TO_BLE, normed_one, tensors[SELF_QKV]) + qkv_bias).astype(
        jnp.bfloat16
    )
    self_query = packed_qkv[..., :model_width].reshape(heads_shape)
    self_keys = packed_qkv[..., model_width : 2 * model_width].reshape(heads_shape)
    self_values = packed_qkv[..., 2 * model_width :].reshape(heads_shape)
    positions = jnp.arange(cap_length)
    causal = (positions[None, :] <= positions[:, None])[None, None]
    present = (positions[None, :] < caption_len[:, None])[:, None, None, :]
    self_allowed = causal & present
    self_probs, self_log = softmax_forward(self_query, self_keys, self_allowed)
    self_mixed = (
        product(E_BHQK_BKHE_TO_BQHE, self_probs.astype(jnp.bfloat16), self_values)
        .reshape(token_layout_form)
        .astype(jnp.bfloat16)
    )
    first_sum = (
        input_values
        + product(E_BLD_DE_TO_BLE, self_mixed, tensors[SELF_OUT])
        + as_float(tensors, SELF_OUT_BIAS)
    )
    normed_two = layer_norm(
        first_sum, as_float(tensors, NORM_TWO_GAIN), as_float(tensors, NORM_TWO_SHIFT)
    ).astype(jnp.bfloat16)
    cross_queries = (
        (
            product(E_BLD_DE_TO_BLE, normed_two, tensors[CROSS_QUERY])
            + as_float(tensors, CROSS_QUERY_BIAS)
        )
        .astype(jnp.bfloat16)
        .reshape(heads_shape)
    )
    kv_bias = jnp.concatenate([zero_part, tensors[CROSS_VALUE_BIAS]]).astype(jnp.float32)
    kv_weight = tensors[CROSS_KV]
    group_kv = (
        product(E_TPD_DE_TO_TPE, lax.all_gather(tiles, FSDP, axis=0, tiled=True), kv_weight)
        + kv_bias
    ).astype(jnp.bfloat16)
    chosen = jnp.stack(
        [
            jnp.stack(
                [
                    lax.dynamic_index_in_dim(group_kv, tile_index[c, s], 0, keepdims=False)
                    for s in range(slot_count)
                ]
            )
            for c in range(caption_rows)
        ]
    )
    cross_keys = chosen[..., :model_width].reshape(key_shape)
    cross_values = chosen[..., model_width:].reshape(key_shape)
    usable = jnp.repeat(tile_valid > 0, patch_count, axis=1)[:, None, None, :]
    cross_probs, cross_log = softmax_forward(cross_queries, cross_keys, usable)
    cross_mixed = (
        product(E_BHQK_BKHE_TO_BQHE, cross_probs.astype(jnp.bfloat16), cross_values)
        .reshape(token_layout_form)
        .astype(jnp.bfloat16)
    )
    second = (
        first_sum
        + product(E_BLD_DE_TO_BLE, cross_mixed, tensors[CROSS_OUT])
        + as_float(tensors, CROSS_OUT_BIAS)
    )
    normed_three = layer_norm(
        second, as_float(tensors, NORM_THREE_GAIN), as_float(tensors, NORM_THREE_SHIFT)
    ).astype(jnp.bfloat16)
    preact = product(E_BLD_DF_TO_BLF, normed_three, tensors[MLP_UP]) + as_float(
        tensors, MLP_UP_BIAS
    )
    activation = gelu_exact(preact).astype(jnp.bfloat16)
    result = (
        second
        + product(E_BLF_FD_TO_BLD, activation, tensors[MLP_DOWN])
        + as_float(tensors, MLP_DOWN_BIAS)
    ).astype(jnp.bfloat16)
    back_flat = lax.all_gather(weights, FSDP, axis=0, tiled=True)
    tensors = unpack(back_flat, model_width, hidden_width)
    gradients = {}
    out_grad = d_out.astype(jnp.float32)
    gradients[MLP_DOWN] = product(E_BLF_BLD_TO_FD, activation, d_out)
    gradients[MLP_DOWN_BIAS] = column_sums(d_out)
    activ_grad = product(E_BLD_FD_TO_BLF, d_out, tensors[MLP_DOWN])
    gelu_value, gelu_pull = jax.vjp(gelu_exact, preact)
    preact_grad = gelu_pull(activ_grad)[0].astype(jnp.bfloat16)
    gradients[MLP_UP] = product(E_BLD_BLF_TO_DF, normed_three, preact_grad)
    gradients[MLP_UP_BIAS] = column_sums(preact_grad)
    second_grad = out_grad + norm_back(
        second,
        tensors,
        NORM_THREE_GAIN,
        NORM_THREE_SHIFT,
        product(E_BLF_DF_TO_BLD, preact_grad, tensors[MLP_UP]),
        gradients,
    )
    cross_branch = second_grad.astype(jnp.bfloat16)
    gradients[CROSS_OUT] = product(E_BLD_BLE_TO_DE, cross_mixed, cross_branch)
    gradients[CROSS_OUT_BIAS] = column_sums(cross_branch)
    cmixed_grad = (
        product(E_BLE_DE_TO_BLD, cross_branch, tensors[CROSS_OUT])
        .astype(jnp.bfloat16)
        .reshape(heads_shape)
    )
    cquery_grad, ckeys_grad, cvalues_grad = attention_backward_pass(
        cross_queries, cross_keys, cross_values, usable, cross_log, cmixed_grad
    )
    cquery_low = cquery_grad.astype(jnp.bfloat16).reshape(token_layout_form)
    gradients[CROSS_QUERY] = product(E_BLD_BLE_TO_DE, normed_two, cquery_low)
    gradients[CROSS_QUERY_BIAS] = column_sums(cquery_low)
    first_grad = second_grad + norm_back(
        first_sum,
        tensors,
        NORM_TWO_GAIN,
        NORM_TWO_SHIFT,
        product(E_BLE_DE_TO_BLD, cquery_low, tensors[CROSS_QUERY]),
        gradients,
    )
    slot_layout_form = (caption_rows, slot_count, patch_count, model_width)
    slot_grad = jnp.concatenate(
        [ckeys_grad.reshape(slot_layout_form), cvalues_grad.reshape(slot_layout_form)], axis=-1
    )
    picked = (tile_index[:, :, None] == jnp.arange(group_kv.shape[0])[None, None, :]).astype(
        jnp.float32
    )
    group_grad = jnp.einsum(E_CSG_CSPE_TO_GPE, picked, slot_grad, precision=lax.Precision.HIGHEST)
    arrived = lax.all_to_all(
        group_grad.astype(jnp.bfloat16), FSDP, split_axis=0, concat_axis=0, tiled=True
    ).astype(group_grad.dtype)
    own_grad = jnp.sum(arrived.reshape((group_size, own_tiles) + arrived.shape[1:]), axis=0).astype(
        jnp.bfloat16
    )
    gradients[CROSS_KV] = product(E_TPD_TPE_TO_DE, tiles, own_grad)
    gradients[CROSS_VALUE_BIAS] = column_sums(own_grad[..., model_width:])
    tiles_grad = product(E_TPE_DE_TO_TPD, own_grad, tensors[CROSS_KV])
    self_branch = first_grad.astype(jnp.bfloat16)
    gradients[SELF_OUT] = product(E_BLD_BLE_TO_DE, self_mixed, self_branch)
    gradients[SELF_OUT_BIAS] = column_sums(self_branch)
    smixed_grad = (
        product(E_BLE_DE_TO_BLD, self_branch, tensors[SELF_OUT])
        .astype(jnp.bfloat16)
        .reshape(heads_shape)
    )
    self_query_gradient, self_key_gradient, self_value_gradient = attention_backward_pass(
        self_query, self_keys, self_values, self_allowed, self_log, smixed_grad
    )
    qkv_grad = jnp.concatenate(
        [
            self_query_gradient.reshape(token_layout_form),
            self_key_gradient.reshape(token_layout_form),
            self_value_gradient.reshape(token_layout_form),
        ],
        axis=-1,
    ).astype(jnp.bfloat16)
    gradients[SELF_QKV] = product(E_BLD_BLE_TO_DE, normed_one, qkv_grad)
    gradients[SELF_QUERY_BIAS] = column_sums(qkv_grad[..., :model_width])
    gradients[SELF_VALUE_BIAS] = column_sums(qkv_grad[..., 2 * model_width :])
    caption_grad = first_grad + norm_back(
        input_values,
        tensors,
        NORM_ONE_GAIN,
        NORM_ONE_SHIFT,
        product(E_BLE_DE_TO_BLD, qkv_grad, tensors[SELF_QKV]),
        gradients,
    )
    flat_grad = pack_rows(gradients, model_width, hidden_width, total_rows)
    shard_rows = total_rows // (data_size * group_size)
    received = lax.all_to_all(
        for_sending(flat_grad), DP, split_axis=0, concat_axis=0, tiled=True
    ).astype(flat_grad.dtype)
    data_grad = jnp.sum(received.reshape(data_size, group_size * shard_rows, 128), axis=0)
    shard_grad = lax.psum_scatter(
        data_grad.astype(jnp.bfloat16), FSDP, scatter_dimension=0, tiled=True
    ).astype(jnp.float32)
    begin_row = lax.axis_index(BOTH) * shard_rows
    seg_starts, seg_ends, decay_flags, seg_entries = segment_table(model_width, hidden_width)
    row_ids = begin_row + jnp.arange(shard_rows)
    member = (row_ids[:, None] >= seg_starts[None, :]) & (row_ids[:, None] < seg_ends[None, :])
    row_squares = jnp.sum(shard_grad * shard_grad, axis=1)
    part_sums = jnp.sum(jnp.where(member, row_squares[:, None], 0.0), axis=0)
    square_sums = lax.psum(part_sums, BOTH)
    old_weights = lax.dynamic_slice_in_dim(back_flat, begin_row, shard_rows, 0).astype(jnp.float32)
    update, new_first, new_second, grad_norm, tensor_rms = adam_step(
        shard_grad,
        member,
        decay_flags,
        old_weights,
        first_moment,
        second_moment,
        square_sums,
        seg_entries,
    )
    return (
        result,
        caption_grad,
        tiles_grad,
        shard_grad,
        update,
        new_first,
        new_second,
        grad_norm,
        tensor_rms,
    )


D = HEADS * HEAD_DIM
NZ = 4
TOK = 128
PATCH = 196
PATCH_SENT = 208
PATCH_SLOT = 256
KEYS = 2 * PATCH_SLOT
LEAD = 80
BF, F32 = jnp.bfloat16, jnp.float32
MESH = pl.DeviceIdType.MESH
SHARD, PIECES, PIECE = 2312, 5, 464
PADDED = PIECES * PIECE
WINDOW = 8 * SHARD
CARRY = 96
SEGS = 24
QKV_AT, WO_AT, UQ_AT, UKV_AT, UO_AT, WIDE = 0, 2304, 3072, 3840, 5376, 6144
W1_AT, W2_AT = 0, 3072
(V_G1, V_C1, V_BQKV, V_BO, V_G2, V_C2, V_UQ, V_BKV, V_UO, V_G3, V_C3, V_B1, V_B2) = range(13)


def row_starts():
    starts, at = {}, 0
    for label, shape, _ in layout(D, FF):
        starts[label] = at
        at += int(np.prod(shape)) // 128
    return starts


def mm(a, b):
    return lax.dot_general(a, b, (((1,), (0,)), ((), ())), preferred_element_type=F32)


def mm_nt(a, b):
    return lax.dot_general(a, b, (((1,), (1,)), ((), ())), preferred_element_type=F32)


def mm_tn(a, b):
    return lax.dot_general(a, b, (((0,), (0,)), ((), ())), preferred_element_type=F32)


def al(i, m):
    return pl.multiple_of(i * m, m)


def halves(pair):
    lane = lax.broadcasted_iota(jnp.int32, pair.shape, 1)
    zero = jnp.zeros_like(pair)
    return jnp.concatenate(
        [jnp.where(lane < HEAD_DIM, pair, zero), jnp.where(lane < HEAD_DIM, zero, pair)], axis=0
    )


def joined(stacked):
    n = stacked.shape[0] // 2
    lane = lax.broadcasted_iota(jnp.int32, (n, 128), 1)
    return jnp.where(lane < HEAD_DIM, stacked[:n], stacked[n:])


def normed(v):
    center = v - jnp.mean(v, axis=-1, keepdims=True)
    r = lax.rsqrt(jnp.mean(center * center, axis=-1, keepdims=True) + EPS_NORM)
    return center * r, r


def pair_kernel(
    cap, tiles, d_out, index, valid, length, weights,
    g_out, sums_out, old_out, out, dcap, dtile,
    fw, wide, gf, pc, ps, big1, big2, kv, dkvt, tl, tlT,
    xin, h1, am, h2, q2, a2, sb, rb, dy, t1, h1T, amT, h2T, a2T,
    x1, dx, acc, vec, meta, ob, pfx, pfx_in, carry, dcap_b, dtile_b,
    from_core, from_y, from_x, from_low, from_high, total, sq,
    wsem, gsem, send, recv, core_s, core_r, y_s, y_r, x_s, x_r, up_s, up_r, down_s, down_r, free, sum_s, sum_r,
):
    role = lax.axis_index(FSDP)
    other = 1 - role
    me = lax.axis_index(DP)
    my_z, my_y, my_core = me // 4, (me // 2) % 2, me % 2

    def at_dp(z, y, core):
        return {DP: z * 4 + y * 2 + core, FSDP: role}

    core_peer = at_dp(my_z, my_y, 1 - my_core)
    y_peer = at_dp(my_z, 1 - my_y, my_core)
    x_peer = {DP: me, FSDP: other}
    up_peer = at_dp(jnp.minimum(my_z + 1, NZ - 1), my_y, my_core)
    down_peer = at_dp(jnp.maximum(my_z - 1, 0), my_y, my_core)
    row0 = row_starts()

    cuts = [0, 13856, 18480, 23088, 32320, weights.shape[0]]
    loads = []
    for i in range(5):
        n = cuts[i + 1] - cuts[i]
        loads.append(
            pltpu.make_async_copy(
                weights.at[pl.ds(cuts[i], n)], fw.at[pl.ds(LEAD + cuts[i], n)], wsem.at[i]
            )
        )
    for c in loads:
        c.start()

    def to_other(src, dst, k):
        return pltpu.make_async_remote_copy(
            src_ref=src, dst_ref=dst, send_sem=send.at[k], recv_sem=recv.at[k],
            device_id=x_peer, device_id_type=MESH,
        )

    first, later = pl.ds(0, TOK), pl.ds(TOK, TOK)
    copies = dict(
        cap=to_other(cap, xin.at[later], 0),
        tile=to_other(tl.at[pl.ds(0, PATCH_SENT)], tl.at[pl.ds(PATCH_SLOT, PATCH_SENT)], 1),
        meta=to_other(meta.at[0], meta.at[1], 2),
        dy=to_other(d_out, dy.at[first], 3),
        lead=to_other(fw.at[pl.ds(weights.shape[0], LEAD)], fw.at[pl.ds(0, LEAD)], 4),
        x2=to_other(sb, rb, 5),
        dx2=to_other(sb, rb, 6),
        out=to_other(t1.at[first], ob, 7),
        pfx=to_other(pfx, pfx_in, 8),
        old=to_other(
            weights.at[pl.ds(pl.multiple_of(((2 * me + other) % 16) * SHARD - 8 * other, 16), PADDED)], old_out, 9
        ),
        dcap=to_other(dcap_b, dcap_b, 10),
        dtile=to_other(dtile_b, dtile_b, 11),
    )

    tl[...] = jnp.zeros_like(tl)
    tl[0:PATCH, :] = tiles[...]
    counts = []
    for g in range(2):
        named_by = jnp.int32(0)
        for s in range(index.shape[1]):
            named = jnp.where(index[0, s] == g, jnp.int32(1), jnp.int32(0))
            named_by = named_by + jnp.where(valid[0, s] > 0, named, jnp.int32(0))
        counts.append(named_by)
    rows8 = lax.broadcasted_iota(jnp.int32, (8, 128), 0)
    meta[0] = jnp.where(
        rows8 == 0, counts[0], jnp.where(rows8 == 1, counts[1], length[0])
    ).astype(F32)

    barrier = pltpu.get_barrier_semaphore()
    for peer in (core_peer, y_peer, x_peer):
        pl.semaphore_signal(barrier, inc=1, device_id=peer, device_id_type=MESH)
    for step in range(1, NZ):
        peer = at_dp((my_z + step) % NZ, my_y, my_core)
        pl.semaphore_signal(barrier, inc=1, device_id=peer, device_id_type=MESH)
    pl.semaphore_wait(barrier, 3 + NZ - 1)

    def vector(row, at, n, col=0):
        block = fw[pl.ds(at, n // 128), :].astype(F32)
        for j in range(n // 128):
            vec[row : row + 1, col + 128 * j : col + 128 * j + 128] = block[j : j + 1, :]

    def widen(at, k, col, rows=D):
        for j in range(k):
            wide[:, col + 128 * j : col + 128 * j + 128] = fw[pl.ds(at + j, rows, stride=k), :]

    def norm_forward(src, dst, g, c):
        @pl.loop(0, 4)
        def _(i):
            rows = pl.ds(al(i, 64), 64)
            n, _ = normed(src[rows, :].astype(F32))
            dst[rows, :] = (n * vec[g : g + 1, :D] + vec[c : c + 1, :D]).astype(BF)

    def norm_backward(src, dh, g, write, g_at, c_at, into):
        sums = (jnp.zeros((1, D), F32), jnp.zeros((1, D), F32))

        def step(i, carry):
            rows = pl.ds(al(i, 64), 64)
            n, r = normed(src[rows, :].astype(F32))
            d = dh[rows, :]
            dn = d * vec[g : g + 1, :D]
            dv = r * (
                dn - jnp.mean(dn, axis=-1, keepdims=True) - n * jnp.mean(dn * n, axis=-1, keepdims=True)
            )
            write(rows, dv)
            return (
                carry[0] + jnp.sum(d * n, axis=0, keepdims=True),
                carry[1] + jnp.sum(d, axis=0, keepdims=True),
            )

        gg, gc = lax.fori_loop(0, 4, step, sums)
        put_vector(g_at, gg, into)
        put_vector(c_at, gc, into)

    def put_vector(at, row, into=gf):
        for j in range(row.shape[1] // 128):
            into[at + j : at + j + 1, :] = row[:, 128 * j : 128 * j + 128]

    def column_total(ref, cols):
        return jnp.sum(ref[:, cols].astype(F32), axis=0, keepdims=True)

    def matrix_grad(at, k, lhs_t, rhs, transposed=False):
        @pl.loop(0, k // 2)
        def _(m):
            cols = pl.ds(al(m, 256), 256)
            res = mm_nt(lhs_t[...], rhs[cols, :]) if transposed else mm(lhs_t[...], rhs[:, cols])
            for half in range(2):
                gf[pl.ds(at + 2 * m + half, D, stride=k), :] = res[:, 128 * half : 128 * half + 128]

    def copy_to(peer, src, dst, ssem, rsem):
        return pltpu.make_async_remote_copy(
            src_ref=src, dst_ref=dst, send_sem=ssem, recv_sem=rsem, device_id=peer, device_id_type=MESH
        )

    def slot(w, s, core, y=0, x=0):
        return pl.multiple_of(((w * PIECES + s) * 8 + core * 4 + y * 2 + x) * PIECE, 16)

    class Scatter:
        def __init__(self, w, x):
            self.w, self.x = w, x

        def core(self, s):
            rows = pl.ds(slot(self.w, s, 1 - my_core), 4 * PIECE)
            return copy_to(core_peer, fw.at[rows], from_core.at[s], core_s.at[s], core_r.at[s])

        def y(self, s):
            rows = pl.ds(slot(self.w, s, my_core, 1 - my_y), 2 * PIECE)
            return copy_to(y_peer, fw.at[rows], from_y.at[s], y_s.at[s], y_r.at[s])

        def over(self, s):
            rows = pl.ds(slot(self.w, s, my_core, my_y, 1 - self.x), PIECE)
            return copy_to(x_peer, fw.at[rows], from_x.at[s], x_s.at[s], x_r.at[s])

        def held(self, s, h):
            if h == self.x:
                return fw.at[pl.ds(slot(self.w, s, my_core, my_y, self.x), PIECE)]
            return from_x.at[s]

        def up(self, s, h):
            return copy_to(up_peer, self.held(s, h), from_low.at[s, h], up_s.at[s, h], up_r.at[s, h])

        def down(self, s, h):
            return copy_to(down_peer, self.held(s, h), from_high.at[s, h], down_s.at[s, h], down_r.at[s, h])

        def cast(self, first_row):
            @pl.loop(0, PIECES)
            def _(s):
                for k in range(8):
                    j = (k & 2) * 2 + (k & 4) // 2 + (k & 1)
                    src = pl.ds(pl.multiple_of(first_row + j * SHARD + s * PIECE, 8), PIECE)
                    fw[pl.ds(pl.multiple_of(slot(self.w, s, 0) + k * PIECE, 16), PIECE), :] = gf[src, :].astype(BF)
                self.core(s).start()

        def add_core(self):
            @pl.loop(0, PIECES)
            def _(s):
                self.core(s).wait_recv()
                rows = pl.ds(slot(self.w, s, my_core), 4 * PIECE)
                fw[rows, :] = fw[rows, :] + from_core[s]

        def start_y(self):
            @pl.loop(0, PIECES)
            def _(s):
                self.y(s).start()

        def add_y(self, s):
            self.y(s).wait_recv()
            rows = pl.ds(slot(self.w, s, my_core, my_y), 2 * PIECE)
            fw[rows, :] = fw[rows, :] + from_y[s]
            self.over(s).start()

        def from_ends(self, s):
            self.over(s).wait_recv()
            for h in range(2):
                goal = 2 * h + self.w
                if goal > 0:
                    pl.when(my_z == 0)(self.up(s, h).start)
                if goal < NZ - 1:
                    pl.when(my_z == NZ - 1)(self.down(s, h).start)

        def relay(self, s):
            for h in range(2):
                goal = 2 * h + self.w
                mine = self.held(s, h)
                if goal > 1:

                    @pl.when((my_z > 0) & (my_z < goal))
                    def _():
                        self.up(s, h).wait_recv()
                        mine[...] = mine[...] + from_low[s, h]
                        self.up(s, h).start()

                if goal < NZ - 2:

                    @pl.when((my_z < NZ - 1) & (my_z > goal))
                    def _():
                        self.down(s, h).wait_recv()
                        mine[...] = mine[...] + from_high[s, h]
                        self.down(s, h).start()

        def collect(self, s):
            for h in range(2):
                goal = 2 * h + self.w

                @pl.when(my_z == goal)
                def _():
                    whole = self.held(s, h)[...].astype(F32)
                    if goal > 0:
                        self.up(s, h).wait_recv()
                        whole = whole + from_low[s, h].astype(F32)
                    if goal < NZ - 1:
                        self.down(s, h).wait_recv()
                        whole = whole + from_high[s, h].astype(F32)
                    total[pl.ds(pl.multiple_of(s * PIECE, 8), PIECE), :] = whole

        def sent(self):
            @pl.loop(0, PIECES)
            def _(s):
                self.core(s).wait_send()
                self.y(s).wait_send()
                self.over(s).wait_send()

        def sent_z(self):
            @pl.loop(0, PIECES)
            def _(s):
                for h in range(2):
                    goal = 2 * h + self.w
                    pl.when(my_z < goal)(self.up(s, h).wait_send)
                    pl.when(my_z > goal)(self.down(s, h).wait_send)

    def give(k, peer):
        pl.semaphore_signal(free.at[k], inc=1, device_id=peer, device_id_type=MESH)

    def take(k):
        pl.semaphore_wait(free.at[k], 1)

    def rest_of_scatter(one, zero):
        @pl.loop(0, PIECES)
        def _(s):
            one.add_y(s)

        give(1, y_peer)
        take(1)
        zero.start_y()

        pl.loop(0, PIECES)(one.from_ends)
        pl.loop(0, PIECES)(one.relay)
        pl.loop(0, PIECES)(one.collect)

        one.sent_z()
        give(2, x_peer)
        pl.when(my_z > 0)(lambda: give(3, down_peer))
        pl.when(my_z < NZ - 1)(lambda: give(4, up_peer))
        take(2)
        pl.when(my_z < NZ - 1)(lambda: take(3))
        pl.when(my_z > 0)(lambda: take(4))

        @pl.loop(0, PIECES)
        def _(s):
            zero.add_y(s)

            pl.when(s > 0)(lambda: zero.from_ends(s - 1))
            pl.when(s > 1)(lambda: zero.relay(s - 2))

        zero.from_ends(PIECES - 1)
        zero.relay(PIECES - 2)
        zero.relay(PIECES - 1)
        pl.loop(0, PIECES)(zero.collect)
        zero.sent()
        zero.sent_z()

    def square_sums():
        total[SHARD:, :] = jnp.zeros((total.shape[0] - SHARD, 128), F32)
        done = pltpu.make_async_copy(total.at[pl.ds(0, SHARD)], g_out, gsem)
        done.start()
        seg = lax.broadcasted_iota(jnp.int32, (SEGS, 1), 0)
        begin = jnp.full((SEGS, 1), 1 << 30, jnp.int32)
        end = begin
        for i, (a, b) in enumerate(zip(*segment_table(D, FF)[:2])):
            begin = jnp.where(seg == i, int(a), begin)
            end = jnp.where(seg == i, int(b), end)
        row = (me * 2 + role) * SHARD + lax.broadcasted_iota(jnp.int32, (SEGS, total.shape[0]), 1)
        member = jnp.where((row >= begin) & (row < end), 1.0, 0.0)
        squares = lax.dot_general(
            member, total[...] * total[...], (((1,), (0,)), ((), ())),
            precision=lax.Precision.HIGHEST, preferred_element_type=F32,
        )
        mine = jnp.broadcast_to(jnp.sum(squares, axis=1, keepdims=True), (SEGS, 128))
        for i, peer in enumerate((core_peer, y_peer, x_peer)):
            sq[2 * i] = mine
            swap = copy_to(peer, sq.at[2 * i], sq.at[2 * i + 1], sum_s.at[i], sum_r.at[i])
            swap.start()
            swap.wait()
            mine = mine + sq[2 * i + 1]
        sq[6] = mine
        sends = []
        for step in range(1, NZ):
            to = at_dp((my_z + step) % NZ, my_y, my_core)
            sends.append(copy_to(to, sq.at[6], sq.at[6 + step], sum_s.at[2 + step], sum_r.at[2 + step]))
            sends[-1].start()
        for c in sends:
            c.wait()
        whole = jnp.zeros((SEGS, 128), F32)
        for z in range(NZ):
            part = mine
            for step in range(1, NZ):
                part = jnp.where((my_z - step + NZ) % NZ == z, sq[6 + step], part)
            whole = whole + part
        sums_out[...] = whole
        done.wait()

    def attention_role():
        at = {k: LEAD + v for k, v in row0.items()}
        at0 = {k: CARRY + v for k, v in row0.items()}
        at1 = {k: CARRY - WINDOW + v for k, v in row0.items()}
        one, zero = Scatter(1, 0), Scatter(0, 0)
        xin[first, :] = cap[...]
        copies["dy"].start()
        loads[0].wait()
        vector(V_G1, at[NORM_ONE_GAIN], D)
        vector(V_C1, at[NORM_ONE_SHIFT], D)
        vec[V_BQKV : V_BQKV + 1, :] = jnp.zeros((1, FF), F32)
        vec[V_BKV : V_BKV + 1, :] = jnp.zeros((1, FF), F32)
        vector(V_BQKV, at[SELF_QUERY_BIAS], D)
        vector(V_BQKV, at[SELF_VALUE_BIAS], D, 2 * D)
        widen(at[SELF_QKV], 18, QKV_AT)
        for c in loads[1:]:
            c.wait()
        copies["lead"].start()
        vector(V_BO, at[SELF_OUT_BIAS], D)
        vector(V_G2, at[NORM_TWO_GAIN], D)
        vector(V_C2, at[NORM_TWO_SHIFT], D)
        vector(V_UQ, at[CROSS_QUERY_BIAS], D)
        vector(V_BKV, at[CROSS_VALUE_BIAS], D, D)
        vector(V_UO, at[CROSS_OUT_BIAS], D)
        widen(at[SELF_OUT], 6, WO_AT)
        widen(at[CROSS_QUERY], 6, UQ_AT)
        widen(at[CROSS_KV], 12, UKV_AT)
        widen(at[CROSS_OUT], 6, UO_AT)

        copies["cap"].wait_recv()
        norm_forward(xin, h1, V_G1, V_C1)

        @pl.loop(0, 3)
        def _(j):
            cols = pl.ds(al(j, D), D)
            big1[:, cols] = (mm(h1[...], wide[:, cols]) + vec[V_BQKV : V_BQKV + 1, cols]).astype(BF)

        copies["meta"].wait_recv()

        @pl.loop(0, 12)
        def _(i):
            c, p = i // 6, i % 6
            rows = pl.ds(al(c, TOK), TOK)
            qq = halves(big1[rows, pl.ds(al(p, 128), 128)]) * BF(0.125)
            k2 = big1[rows, pl.ds(al(p, 128) + D, 128)]
            v2 = big1[rows, pl.ds(al(p, 128) + 2 * D, 128)]
            s = mm_nt(qq, k2)
            row = lax.broadcasted_iota(jnp.int32, s.shape, 0) % TOK
            col = lax.broadcasted_iota(jnp.int32, s.shape, 1)
            present = col.astype(F32) < meta[c][2:3, :]
            s = jnp.where((col <= row) & present, s, NEG_LARGE)
            e = jnp.exp(s - jnp.max(s, axis=-1, keepdims=True))
            prob = (e / jnp.sum(e, axis=-1, keepdims=True)).astype(BF)
            ps[i] = prob
            am[rows, pl.ds(al(p, 128), 128)] = joined(mm(prob, v2)).astype(BF)

        x1[...] = xin[...].astype(F32) + mm(am[...], wide[:, WO_AT : WO_AT + D]) + vec[V_BO : V_BO + 1, :D]
        norm_forward(x1, h2, V_G2, V_C2)
        q2[...] = (mm(h2[...], wide[:, UQ_AT : UQ_AT + D]) + vec[V_UQ : V_UQ + 1, :D]).astype(BF)
        copies["tile"].wait_recv()

        @pl.loop(0, 2)
        def _(j):
            cols = pl.ds(al(j, D), D)
            kv[:, cols] = (
                mm(tl[...], wide[:, pl.ds(al(j, D) + UKV_AT, D)]) + vec[V_BKV : V_BKV + 1, cols]
            ).astype(BF)

        @pl.loop(0, 12)
        def _(i):
            p, c = i // 2, i % 2
            rows = pl.ds(al(c, TOK), TOK)
            qq = halves(q2[rows, pl.ds(al(p, 128), 128)]) * BF(0.125)
            s = mm_nt(qq, kv[:, pl.ds(al(p, 128), 128)])
            col = lax.broadcasted_iota(jnp.int32, (1, KEYS), 1)
            m = meta[c]
            c0 = jnp.concatenate([m[0:1, :]] * (KEYS // 128), axis=1)
            c1 = jnp.concatenate([m[1:2, :]] * (KEYS // 128), axis=1)
            count = jnp.where(col < PATCH, c0, jnp.where(col < PATCH_SLOT, 0.0, c1))
            count = jnp.where(col < PATCH_SLOT + PATCH, count, 0.0)
            s = jnp.where(count > 0.0, s, NEG_LARGE)
            e = jnp.exp(s - jnp.max(s, axis=-1, keepdims=True)) * count
            prob = (e / jnp.sum(e, axis=-1, keepdims=True)).astype(BF)
            pc[pl.ds(al(i, 2 * TOK), 2 * TOK), :] = prob
            a2[rows, pl.ds(al(p, 128), 128)] = joined(
                mm(prob, kv[:, pl.ds(al(p, 128) + D, 128)])
            ).astype(BF)

        sb[...] = (
            x1[...] + mm(a2[...], wide[:, UO_AT : UO_AT + D]) + vec[V_UO : V_UO + 1, :D]
        ).astype(BF)
        copies["x2"].start()
        copies["old"].start()

        h1T[...] = h1[...].T
        amT[...] = am[...].T
        h2T[...] = h2[...].T
        a2T[...] = a2[...].T
        tlT[...] = tl[...].T

        copies["dx2"].wait_recv()
        t1[...] = mm_nt(rb[...], wide[:, UO_AT : UO_AT + D]).astype(BF)
        put_vector(at1[CROSS_OUT_BIAS], column_total(rb, slice(None)))
        matrix_grad(at1[CROSS_OUT], 6, a2T, rb)

        @pl.loop(0, 6)
        def _(p):
            lanes, vlanes = pl.ds(al(p, 128), 128), pl.ds(al(p, 128) + D, 128)
            dk = dv = None
            for c in range(2):
                rows = pl.ds(c * TOK, TOK)
                qq = halves(q2[rows, lanes]) * BF(0.125)
                do = halves(t1[rows, lanes])
                prob = pc[pl.ds(al(2 * p + c, 2 * TOK), 2 * TOK), :]
                pf = prob.astype(F32)
                dp = mm_nt(do, kv[:, vlanes])
                ds = (pf * (dp - jnp.sum(pf * dp, axis=-1, keepdims=True))).astype(BF)
                am[rows, lanes] = (joined(mm(ds, kv[:, lanes])) * 0.125).astype(BF)
                dk_c, dv_c = mm_tn(qq, ds), mm_tn(do, prob)
                dk, dv = (dk_c, dv_c) if c == 0 else (dk + dk_c, dv + dv_c)
            dkvt[lanes, :] = dk.astype(BF)
            dkvt[vlanes, :] = dv.astype(BF)

        put_vector(at1[CROSS_QUERY_BIAS], column_total(am, slice(None)))
        matrix_grad(at1[CROSS_QUERY], 6, h2T, am)
        acc[...] = mm_nt(am[...], wide[:, UQ_AT : UQ_AT + D])

        def write_dx1(rows, dv):
            full = rb[rows, :].astype(F32) + dv
            dx[rows, :] = full
            sb_[rows, :] = full.astype(BF)

        sb_ = h2
        norm_backward(x1, acc, V_G2, write_dx1, at1[NORM_TWO_GAIN], at1[NORM_TWO_SHIFT], gf)
        matrix_grad(at1[CROSS_KV], 12, tlT, dkvt, transposed=True)
        kv[...] = dkvt[...].T
        put_vector(at1[CROSS_VALUE_BIAS], column_total(kv, slice(D, 2 * D)))

        def tile_grad(rows):
            keys = mm_nt(kv[rows, 0:D], wide[:, UKV_AT : UKV_AT + D])
            return keys + mm_nt(kv[rows, D : 2 * D], wide[:, UKV_AT + D : UKV_AT + 2 * D])

        dtile[...] = tile_grad(pl.ds(0, PATCH_SENT))[:PATCH]
        dtile_b[...] = tile_grad(pl.ds(PATCH_SLOT, PATCH_SENT)).astype(BF)
        copies["dtile"].start()
        copies["pfx"].wait_recv()
        gf[pl.ds(at1[NORM_THREE_GAIN], LEAD - 12), :] = pfx_in[12:, :]
        copies["lead"].wait_send()
        one.cast(CARRY)
        carry[...] = gf[0:CARRY, :]
        put_vector(at0[SELF_OUT_BIAS], column_total(sb_, slice(None)))
        matrix_grad(at0[SELF_OUT], 6, amT, sb_)
        t1[...] = mm_nt(sb_[...], wide[:, WO_AT : WO_AT + D]).astype(BF)

        one.add_core()
        one.start_y()
        give(0, core_peer)

        @pl.loop(0, 12)
        def _(i):
            c, p = i // 6, i % 6
            rows = pl.ds(al(c, TOK), TOK)
            lanes = pl.ds(al(p, 128), 128)
            klanes, vlanes = pl.ds(al(p, 128) + D, 128), pl.ds(al(p, 128) + 2 * D, 128)
            qq = halves(big1[rows, lanes]) * BF(0.125)
            do = halves(t1[rows, lanes])
            prob = ps[i]
            pf = prob.astype(F32)
            dp = mm_nt(do, big1[rows, vlanes])
            ds = (pf * (dp - jnp.sum(pf * dp, axis=-1, keepdims=True))).astype(BF)
            big2[rows, lanes] = (joined(mm(ds, big1[rows, klanes])) * 0.125).astype(BF)
            big2[rows, klanes] = mm_tn(ds, qq).astype(BF)
            big2[rows, vlanes] = mm_tn(prob, do).astype(BF)

        for j in range(3):
            part = mm_nt(big2[:, D * j : D * j + D], wide[:, D * j : D * j + D])
            acc[...] = part if j == 0 else acc[...] + part

        def write_dx0(rows, dv):
            dx[rows, :] = dx[rows, :] + dv

        norm_backward(xin, acc, V_G1, write_dx0, at0[NORM_ONE_GAIN], at0[NORM_ONE_SHIFT], gf)
        dcap[...] = dx[first, :]
        dcap_b[...] = dx[later, :].astype(BF)
        copies["dcap"].start()
        put_vector(at0[SELF_QUERY_BIAS], column_total(big2, slice(0, D)))
        put_vector(at0[SELF_VALUE_BIAS], column_total(big2, slice(2 * D, 3 * D)))
        matrix_grad(at0[SELF_QKV], 18, h1T, big2)
        gf[pl.ds(at0[NORM_TWO_GAIN], WINDOW - row0[NORM_TWO_GAIN]), :] = carry[
            row0[NORM_TWO_GAIN] - WINDOW + CARRY :, :
        ]
        take(0)
        zero.cast(CARRY)
        zero.add_core()
        rest_of_scatter(one, zero)
        one.sent()
        copies["out"].wait_recv()
        out[...] = ob[...]
        for name in ("dy", "x2", "dcap", "dtile"):
            copies[name].wait_send()
        copies["old"].wait()
        square_sums()

    def mlp_role():
        copies["cap"].start()
        copies["tile"].start()
        copies["meta"].start()
        base = LEAD - weights.shape[0]
        at = {k: base + v for k, v in row0.items()}
        at0 = {k: CARRY - weights.shape[0] + v for k, v in row0.items()}
        at1 = {k: v - WINDOW for k, v in at0.items()}
        one, zero = Scatter(1, 1), Scatter(0, 1)
        dy[later, :] = d_out[...]
        for c in loads:
            c.wait()
        for b in range(4):
            widen(at[MLP_DOWN] + 6 * D * b, 6, W2_AT + D * b)
        copies["lead"].wait_recv()
        widen(at[MLP_UP], 24, W1_AT)
        vector(V_G3, at[NORM_THREE_GAIN], D)
        vector(V_C3, at[NORM_THREE_SHIFT], D)
        vector(V_B1, at[MLP_UP_BIAS], FF)
        vector(V_B2, at[MLP_DOWN_BIAS], D)
        copies["dy"].wait_recv()

        @pl.loop(0, 4)
        def _(b):
            dg = mm_nt(dy[...], wide[:, pl.ds(al(b, D) + W2_AT, D)])
            for j in range(6):
                gf[pl.ds(al(6 * b + j, 256), 256), :] = dg[:, 128 * j : 128 * j + 128]

        copies["x2"].wait_recv()
        norm_forward(rb, h1, V_G3, V_C3)
        acc[...] = jnp.zeros_like(acc)

        @pl.loop(0, 4)
        def _(b):
            cols = pl.ds(al(b, D), D)
            x1[...] = mm(h1[...], wide[:, cols]) + vec[V_B1 : V_B1 + 1, cols]

            @pl.loop(0, 8)
            def _(i):
                rows = pl.ds(al(i, 32), 32)
                for j in range(6):
                    z = x1[rows, 128 * j : 128 * j + 128]
                    phi = 0.5 + 0.5 * lax.erf(z * np.float32(np.sqrt(0.5)))
                    dens = jnp.exp(-0.5 * z * z) * np.float32(1.0 / np.sqrt(2.0 * np.pi))
                    lanes = pl.ds(al(b, D) + 128 * j, 128)
                    big1[rows, lanes] = (z * phi).astype(BF)
                    dg = gf[pl.ds(al(6 * b + j, 256) + al(i, 32), 32), :]
                    big2[rows, lanes] = (dg * (phi + z * dens)).astype(BF)

            acc[...] = acc[...] + mm_nt(big2[:, cols], wide[:, cols])

        def write_dx2(rows, dv):
            sb[rows, :] = (dy[rows, :].astype(F32) + dv).astype(BF)

        norm_backward(rb, acc, V_G3, write_dx2, 12, 18, pfx)
        copies["dx2"].start()

        h1T[...] = h1[...].T
        pfx[0:12, :] = jnp.zeros((12, 128), F32)
        for b in range(4):
            head = mm(h1T[0:8, :], big2[:, D * b : D * b + D])
            for r in range(3):
                for j in range(6):
                    row = 24 + 24 * r + 6 * b + j
                    if row < LEAD:
                        pfx[row : row + 1, :] = head[r : r + 1, 128 * j : 128 * j + 128]
        copies["pfx"].start()
        copies["old"].start()

        acc[...] = rb[...].astype(F32) + vec[V_B2 : V_B2 + 1, :D]

        @pl.loop(0, 4)
        def _(b):
            cols = pl.ds(al(b, D), D)
            acc[...] = acc[...] + mm(big1[:, cols], wide[:, pl.ds(al(b, D) + W2_AT, D)])
            pc[pl.ds(al(b, D), D), 0:256] = big1[:, cols].T

        t1[first, :] = acc[first, :].astype(BF)
        copies["out"].start()
        out[...] = acc[later, :].astype(BF)
        gf[pl.ds(at1[MLP_DOWN_BIAS] + 6, WINDOW + CARRY - at1[MLP_DOWN_BIAS] - 6), :] = jnp.zeros(
            (WINDOW + CARRY - at1[MLP_DOWN_BIAS] - 6, 128), F32
        )
        put_vector(at1[MLP_DOWN_BIAS], column_total(dy, slice(None)))
        for b in range(4):
            matrix_grad(at1[MLP_DOWN] + 6 * D * b, 6, pc.at[pl.ds(D * b, D), pl.ds(0, 256)], dy)
        one.cast(CARRY)
        carry[...] = gf[0:CARRY, :]
        put_vector(at0[MLP_UP_BIAS], column_total(big2, slice(None)))
        matrix_grad(at0[MLP_UP], 24, h1T, big2)
        one.add_core()
        one.start_y()
        give(0, core_peer)
        gf[pl.ds(at0[MLP_DOWN], CARRY), :] = carry[...]
        take(0)
        zero.cast(CARRY)
        zero.add_core()
        rest_of_scatter(one, zero)
        one.sent()
        copies["dtile"].wait_recv()
        dtile[...] = dtile_b[0:PATCH, :].astype(F32)
        copies["dcap"].wait_recv()
        dcap[...] = dcap_b[...].astype(F32)
        for name in ("cap", "tile", "meta", "dx2", "pfx", "out"):
            copies[name].wait_send()
        copies["old"].wait()
        square_sums()

    pl.when(role == 0)(attention_role)
    pl.when(role == 1)(mlp_role)


def pair_call(cap, tiles, d_out, index, valid, length, weights):
    vm = pl.BlockSpec(memory_space=pltpu.VMEM)
    sm = pl.BlockSpec(memory_space=pltpu.SMEM)
    hbm = pl.BlockSpec(memory_space=pl.ANY)
    S = jax.ShapeDtypeStruct
    dma, both = pltpu.SemaphoreType.DMA, 2 * TOK

    def bf(*s):
        return pltpu.VMEM(s, BF)

    def fl(*s):
        return pltpu.VMEM(s, F32)

    return pl.pallas_call(
        pair_kernel,
        in_specs=[vm, vm, vm, sm, sm, sm, hbm],
        out_specs=[hbm, vm, hbm, vm, vm, vm],
        out_shape=[
            S((SHARD, 128), F32),
            S((SEGS, 128), F32),
            S((PADDED, 128), BF),
            S((TOK, D), BF),
            S((TOK, D), F32),
            S((PATCH, D), F32),
        ],
        scratch_shapes=[
            bf(16 * PADDED, 128), bf(D, WIDE), fl(CARRY + WINDOW + 8, 128), bf(12 * both, KEYS),
            bf(12, both, 128), bf(both, FF), bf(both, FF), bf(KEYS, 2 * D), bf(2 * D, KEYS), bf(KEYS, D), bf(D, KEYS),
            *[bf(both, D) for _ in range(10)],
            *[bf(D, both) for _ in range(4)],
            *[fl(both, D) for _ in range(3)],
            fl(16, FF), fl(2, 8, 128), bf(TOK, D), fl(LEAD, 128), fl(LEAD, 128), fl(CARRY, 128),
            bf(TOK, D), bf(PATCH_SENT, D),
            bf(PIECES, 4 * PIECE, 128), bf(PIECES, 2 * PIECE, 128), bf(PIECES, PIECE, 128),
            bf(PIECES, 2, PIECE, 128), bf(PIECES, 2, PIECE, 128), fl(2432, 128), fl(10, SEGS, 128),
            dma((5,)), dma, dma((12,)), dma((12,)),
            *[dma((PIECES,)) for _ in range(6)],
            *[dma((PIECES, 2)) for _ in range(4)],
            pltpu.SemaphoreType.REGULAR((5,)), dma((6,)), dma((6,)),
        ],
        compiler_params=pltpu.CompilerParams(
            collective_id=0, has_side_effects=True, vmem_limit_bytes=63 * 2**20
        ),
    )(cap, tiles, d_out, index, valid, length, weights)


def finish(shard_grad, old_weights, first_moment, second_moment, square_sums):
    shard_rows = shard_grad.shape[0]
    begin_row = lax.axis_index(BOTH) * shard_rows
    seg_starts, seg_ends, decay_flags, seg_entries = segment_table(D, FF)
    row_ids = begin_row + jnp.arange(shard_rows)
    member = (row_ids[:, None] >= seg_starts[None, :]) & (row_ids[:, None] < seg_ends[None, :])
    return adam_step(
        shard_grad, member, decay_flags, old_weights, first_moment, second_moment, square_sums, seg_entries
    )


def pair_body(
    captions, tiles, tile_index, tile_valid, caption_len, weights, first_moment, second_moment, d_out
):
    me, f = lax.axis_index(DP), lax.axis_index(FSDP)
    shard_grad, sums, old, out, caption_grad, tiles_grad = pair_call(
        captions[0], tiles[0], d_out[0], tile_index, tile_valid, caption_len, weights
    )
    own = lax.dynamic_slice_in_dim(weights, ((2 * me + f) % 16) * SHARD, SHARD, 0)
    old = lax.dynamic_slice_in_dim(old, 8 * f, SHARD, 0)
    old_weights = jnp.where(me // 8 == f, own, old).astype(jnp.float32)
    update, new_first, new_second, grad_norm, tensor_rms = finish(
        shard_grad, old_weights, first_moment, second_moment, sums[:21, 0]
    )
    return (
        out[None], caption_grad[None], tiles_grad[None], shard_grad, update, new_first, new_second,
        grad_norm, tensor_rms,
    )


def solution(mesh):
    placed = (
        P(BOTH, None, None),
        P(BOTH, None, None),
        P(BOTH, None),
        P(BOTH, None),
        P(BOTH),
        P(FSDP, None),
        P(BOTH, None),
        P(BOTH, None),
        P(BOTH, None, None),
    )
    return jax.shard_map(
        pair_body if mesh.shape[FSDP] == 2 else body,
        mesh=mesh,
        in_specs=placed,
        out_specs=(
            P(BOTH, None, None),
            P(BOTH, None, None),
            P(BOTH, None, None),
            P(BOTH, None),
            P(BOTH, None),
            P(BOTH, None),
            P(BOTH, None),
            P(),
            P(),
        ),
        check_vma=False,
    )
```

profile of v0, /device:TPU:0, one launch (start us, length us, event | category | flops | bytes accessed | tf_op | source)
XLA Modules:
  0.0 210.1 jit_solution(7773553351191228395)
XLA Ops:
  0.7 0.8 and_reduce_fusion
  2.2 0.0 copy-start.4
  2.2 196.2 %shard_map.196 = (f32[2312,128]{1,0:T(8,128)}, f32[24,128]{1,0:T(8,128)}, bf16[2320,128]{1,0:T(8,128)(2,1)}, bf16[128,768]{1,0:T(8,128)(2,1)}, f32[128,768]{1,0:T(8,128)}, /*index=5*/f32[196,768]{1,0:T(8,128)}) custom-call(bf16[128,768]{1,0:T(8,128)(2,1)} %bitcast.10, bf16[196,768]{1,0:T(8,128)(2,1)} %bitcast.8, bf16[128,768]{1,0:T(8,128)(2,1)} %bitcast.11, ...), custom_call_target="tpu_custom_call" | custom-call | tf_op jit(solution)/shard_map/pallas_call | solution.py:1161
  198.4 0.0 copy-done.4
  198.4 1.3 sqrt_reduce_fusion
  200.5 0.0 copy-start.1
  200.5 4.5 %add_multiply_fusion = (f32[2312,128]{1,0:T(8,128)}, f32[2312,128]{1,0:T(8,128)}, f32[2312,128]{1,0:T(8,128)}) fusion(bf16[2320,128]{1,0:T(8,128)(2,1)} %get-tuple-element.20, s32[]{:T(128)S(6)} %select_n.33, bf16[36992,128]{1,0:T(8,128)(2,1)} %weights.1, s32[]{:T(128)S(6)} %select_n.32, pred[2312]{0:T(1024)(128)(4,1)S(1)} %and_reduce_fusion, pred[]{:T(512)S(6)} %eq.5, ...), kind=kLoop, calls=%fused_computation.2 | loop fusion | flops 5326848 | bytes 8288533 | tf_op jit(solution)/shard_map/mul | solution.py:193
  205.0 0.0 copy-start.3
  205.0 0.0 copy-start.2
  205.0 0.0 copy-done.1
  205.0 0.0 copy-start
  205.0 1.4 copy.24
  206.5 0.0 copy-done.3
  206.5 0.7 copy.29
  207.2 0.0 copy-done.2
  207.2 0.7 copy.30
  207.9 0.0 copy-done
  207.9 1.0 copy.31
  (1 shorter events, 0.0 us)
Async XLA Ops:
  2.2 196.2 %copy-start.4 = (f32[21,1]{1,0:T(8,128)S(1)}, f32[21,1]{1,0:T(8,128)}, u32[]{:S(2)}) copy-start(f32[21,1]{1,0:T(8,128)} %constant.96) | copy-start | bytes 256
  200.5 4.6 %copy-start.1 = (f32[196,768]{1,0:T(8,128)S(1)}, f32[196,768]{1,0:T(8,128)}, u32[]{:S(2)}) copy-start(f32[196,768]{1,0:T(8,128)} %get-tuple-element.17) | copy-start | bytes 1806340
  205.0 1.5 copy-start.3
  205.0 2.1 %copy-start.2 = (f32[128,768]{1,0:T(8,128)S(1)}, f32[128,768]{1,0:T(8,128)}, u32[]{:S(2)}) copy-start(f32[128,768]{1,0:T(8,128)} %get-tuple-element.16) | copy-start | bytes 1179652
  205.0 2.9 %copy-start = (f32[2312,128]{1,0:T(8,128)S(1)}, f32[2312,128]{1,0:T(8,128)}, u32[]{:S(2)}) copy-start(f32[2312,128]{1,0:T(8,128)} %get-tuple-element.65) | copy-start | bytes 3551236
where the time goes:
time: 210 us
  Pallas kernels  196 us (93%)
  other arithmetic  6.73 us (3%)
  local copies, waits for them, and re-layouts  3.9 us (2%)
  between operations  3.26 us (2%)
    pallas_call x1, Pallas kernels, pair_call(): pl.pallas_call(pair_kernel, in_specs=[vm, vm, vm, sm, sm, sm, hbm], out_s...  196 us
    mul x1, other arithmetic, adam_step(): -LEARN_RATE  4.54 us

commit v1 on v0

--- a/solution.py
+++ b/solution.py
@@ -1,3 +1,5 @@
+import functools
+
 import jax
 import jax.numpy as jnp
 import numpy as np
@@ -447,7 +449,7 @@
 SEGS = 24
 QKV_AT, WO_AT, UQ_AT, UKV_AT, UO_AT, WIDE = 0, 2304, 3072, 3840, 5376, 6144
 W1_AT, W2_AT = 0, 3072
-(V_G1, V_C1, V_BQKV, V_BO, V_G2, V_C2, V_UQ, V_BKV, V_UO, V_G3, V_C3, V_B1, V_B2) = range(13)
+(V_G1, V_C1, V_BQKV, V_BO, V_G2, V_C2, V_UQ, V_BKV, V_UO, V_G3, V_C3, V_B1, V_B2, V_SUMS) = range(14)
 
 
 def row_starts():
@@ -543,8 +545,6 @@
         meta=to_other(meta.at[0], meta.at[1], 2),
         dy=to_other(d_out, dy.at[first], 3),
         lead=to_other(fw.at[pl.ds(weights.shape[0], LEAD)], fw.at[pl.ds(0, LEAD)], 4),
-        x2=to_other(sb, rb, 5),
-        dx2=to_other(sb, rb, 6),
         out=to_other(t1.at[first], ob, 7),
         pfx=to_other(pfx, pfx_in, 8),
         old=to_other(
@@ -553,6 +553,16 @@
         dcap=to_other(dcap_b, dcap_b, 10),
         dtile=to_other(dtile_b, dtile_b, 11),
     )
+
+    def to_other_half(c, k):
+        rows = pl.ds(al(c, TOK), TOK)
+        return to_other(sb.at[rows], rb.at[rows], k + c)
+
+    def x2_copy(c):
+        return to_other_half(c, 12)
+
+    def dx2_copy(c):
+        return to_other_half(c, 14)
 
     tl[...] = jnp.zeros_like(tl)
     tl[0:PATCH, :] = tiles[...]
@@ -585,33 +595,29 @@
         for j in range(k):
             wide[:, col + 128 * j : col + 128 * j + 128] = fw[pl.ds(at + j, rows, stride=k), :]
 
-    def norm_forward(src, dst, g, c):
-        @pl.loop(0, 4)
+    def norm_forward(src, dst, g, c, at=0, n=2 * TOK):
+        @pl.loop(0, n // 64)
         def _(i):
-            rows = pl.ds(al(i, 64), 64)
-            n, _ = normed(src[rows, :].astype(F32))
-            dst[rows, :] = (n * vec[g : g + 1, :D] + vec[c : c + 1, :D]).astype(BF)
-
-    def norm_backward(src, dh, g, write, g_at, c_at, into):
-        sums = (jnp.zeros((1, D), F32), jnp.zeros((1, D), F32))
-
-        def step(i, carry):
-            rows = pl.ds(al(i, 64), 64)
-            n, r = normed(src[rows, :].astype(F32))
+            rows = pl.ds(pl.multiple_of(at + 64 * i, 64), 64)
+            v, _ = normed(src[rows, :].astype(F32))
+            dst[rows, :] = (v * vec[g : g + 1, :D] + vec[c : c + 1, :D]).astype(BF)
+
+    def norm_backward(src, dh, g, write, at=0, n=2 * TOK):
+        def step(i, sums):
+            rows = pl.ds(pl.multiple_of(at + 64 * i, 64), 64)
+            v, r = normed(src[rows, :].astype(F32))
             d = dh[rows, :]
             dn = d * vec[g : g + 1, :D]
             dv = r * (
-                dn - jnp.mean(dn, axis=-1, keepdims=True) - n * jnp.mean(dn * n, axis=-1, keepdims=True)
+                dn - jnp.mean(dn, axis=-1, keepdims=True) - v * jnp.mean(dn * v, axis=-1, keepdims=True)
             )
             write(rows, dv)
             return (
-                carry[0] + jnp.sum(d * n, axis=0, keepdims=True),
-                carry[1] + jnp.sum(d, axis=0, keepdims=True),
+                sums[0] + jnp.sum(d * v, axis=0, keepdims=True),
+                sums[1] + jnp.sum(d, axis=0, keepdims=True),
             )
 
-        gg, gc = lax.fori_loop(0, 4, step, sums)
-        put_vector(g_at, gg, into)
-        put_vector(c_at, gc, into)
+        return lax.fori_loop(0, n // 64, step, (jnp.zeros((1, D), F32), jnp.zeros((1, D), F32)))
 
     def put_vector(at, row, into=gf):
         for j in range(row.shape[1] // 128):
@@ -642,26 +648,30 @@
 
         def core(self, s):
             rows = pl.ds(slot(self.w, s, 1 - my_core), 4 * PIECE)
-            return copy_to(core_peer, fw.at[rows], from_core.at[s], core_s.at[s], core_r.at[s])
+            return copy_to(core_peer, fw.at[rows], from_core.at[s], core_s.at[self.w, s], core_r.at[self.w, s])
 
         def y(self, s):
             rows = pl.ds(slot(self.w, s, my_core, 1 - my_y), 2 * PIECE)
-            return copy_to(y_peer, fw.at[rows], from_y.at[s], y_s.at[s], y_r.at[s])
+            return copy_to(y_peer, fw.at[rows], from_y.at[self.w, s], y_s.at[self.w, s], y_r.at[self.w, s])
 
         def over(self, s):
             rows = pl.ds(slot(self.w, s, my_core, my_y, 1 - self.x), PIECE)
-            return copy_to(x_peer, fw.at[rows], from_x.at[s], x_s.at[s], x_r.at[s])
+            return copy_to(x_peer, fw.at[rows], from_x.at[self.w, s], x_s.at[self.w, s], x_r.at[self.w, s])
 
         def held(self, s, h):
             if h == self.x:
                 return fw.at[pl.ds(slot(self.w, s, my_core, my_y, self.x), PIECE)]
-            return from_x.at[s]
+            return from_x.at[self.w, s]
 
         def up(self, s, h):
-            return copy_to(up_peer, self.held(s, h), from_low.at[s, h], up_s.at[s, h], up_r.at[s, h])
+            return copy_to(
+                up_peer, self.held(s, h), from_low.at[self.w, s, h], up_s.at[self.w, s, h], up_r.at[self.w, s, h]
+            )
 
         def down(self, s, h):
-            return copy_to(down_peer, self.held(s, h), from_high.at[s, h], down_s.at[s, h], down_r.at[s, h])
+            return copy_to(
+                down_peer, self.held(s, h), from_high.at[self.w, s, h], down_s.at[self.w, s, h], down_r.at[self.w, s, h]
+            )
 
         def cast(self, first_row):
             @pl.loop(0, PIECES)
@@ -687,7 +697,7 @@
         def add_y(self, s):
             self.y(s).wait_recv()
             rows = pl.ds(slot(self.w, s, my_core, my_y), 2 * PIECE)
-            fw[rows, :] = fw[rows, :] + from_y[s]
+            fw[rows, :] = fw[rows, :] + from_y[self.w, s]
             self.over(s).start()
 
         def from_ends(self, s):
@@ -708,7 +718,7 @@
                     @pl.when((my_z > 0) & (my_z < goal))
                     def _():
                         self.up(s, h).wait_recv()
-                        mine[...] = mine[...] + from_low[s, h]
+                        mine[...] = mine[...] + from_low[self.w, s, h]
                         self.up(s, h).start()
 
                 if goal < NZ - 2:
@@ -716,7 +726,7 @@
                     @pl.when((my_z < NZ - 1) & (my_z > goal))
                     def _():
                         self.down(s, h).wait_recv()
-                        mine[...] = mine[...] + from_high[s, h]
+                        mine[...] = mine[...] + from_high[self.w, s, h]
                         self.down(s, h).start()
 
         def collect(self, s):
@@ -728,10 +738,10 @@
                     whole = self.held(s, h)[...].astype(F32)
                     if goal > 0:
                         self.up(s, h).wait_recv()
-                        whole = whole + from_low[s, h].astype(F32)
+                        whole = whole + from_low[self.w, s, h].astype(F32)
                     if goal < NZ - 1:
                         self.down(s, h).wait_recv()
-                        whole = whole + from_high[s, h].astype(F32)
+                        whole = whole + from_high[self.w, s, h].astype(F32)
                     total[pl.ds(pl.multiple_of(s * PIECE, 8), PIECE), :] = whole
 
         def sent(self):
@@ -740,55 +750,28 @@
                 self.core(s).wait_send()
                 self.y(s).wait_send()
                 self.over(s).wait_send()
-
-        def sent_z(self):
-            @pl.loop(0, PIECES)
-            def _(s):
                 for h in range(2):
                     goal = 2 * h + self.w
                     pl.when(my_z < goal)(self.up(s, h).wait_send)
                     pl.when(my_z > goal)(self.down(s, h).wait_send)
 
-    def give(k, peer):
-        pl.semaphore_signal(free.at[k], inc=1, device_id=peer, device_id_type=MESH)
-
-    def take(k):
-        pl.semaphore_wait(free.at[k], 1)
-
     def rest_of_scatter(one, zero):
-        @pl.loop(0, PIECES)
-        def _(s):
-            one.add_y(s)
-
-        give(1, y_peer)
-        take(1)
         zero.start_y()
-
+        pl.loop(0, PIECES)(one.add_y)
         pl.loop(0, PIECES)(one.from_ends)
-        pl.loop(0, PIECES)(one.relay)
-        pl.loop(0, PIECES)(one.collect)
-
-        one.sent_z()
-        give(2, x_peer)
-        pl.when(my_z > 0)(lambda: give(3, down_peer))
-        pl.when(my_z < NZ - 1)(lambda: give(4, up_peer))
-        take(2)
-        pl.when(my_z < NZ - 1)(lambda: take(3))
-        pl.when(my_z > 0)(lambda: take(4))
 
         @pl.loop(0, PIECES)
         def _(s):
             zero.add_y(s)
-
+            one.relay(s)
             pl.when(s > 0)(lambda: zero.from_ends(s - 1))
-            pl.when(s > 1)(lambda: zero.relay(s - 2))
 
         zero.from_ends(PIECES - 1)
-        zero.relay(PIECES - 2)
-        zero.relay(PIECES - 1)
+        pl.loop(0, PIECES)(zero.relay)
+        pl.loop(0, PIECES)(one.collect)
         pl.loop(0, PIECES)(zero.collect)
+        one.sent()
         zero.sent()
-        zero.sent_z()
 
     def square_sums():
         total[SHARD:, :] = jnp.zeros((total.shape[0] - SHARD, 128), F32)
@@ -869,7 +852,7 @@
 
         copies["meta"].wait_recv()
 
-        @pl.loop(0, 12)
+        @pl.loop(0, 12, unroll=4)
         def _(i):
             c, p = i // 6, i % 6
             rows = pl.ds(al(c, TOK), TOK)
@@ -882,7 +865,7 @@
             present = col.astype(F32) < meta[c][2:3, :]
             s = jnp.where((col <= row) & present, s, NEG_LARGE)
             e = jnp.exp(s - jnp.max(s, axis=-1, keepdims=True))
-            prob = (e / jnp.sum(e, axis=-1, keepdims=True)).astype(BF)
+            prob = (e * (1.0 / jnp.sum(e, axis=-1, keepdims=True))).astype(BF)
             ps[i] = prob
             am[rows, pl.ds(al(p, 128), 128)] = joined(mm(prob, v2)).astype(BF)
 
@@ -898,30 +881,33 @@
                 mm(tl[...], wide[:, pl.ds(al(j, D) + UKV_AT, D)]) + vec[V_BKV : V_BKV + 1, cols]
             ).astype(BF)
 
-        @pl.loop(0, 12)
-        def _(i):
-            p, c = i // 2, i % 2
+        @pl.loop(0, 2)
+        def _(c):
             rows = pl.ds(al(c, TOK), TOK)
-            qq = halves(q2[rows, pl.ds(al(p, 128), 128)]) * BF(0.125)
-            s = mm_nt(qq, kv[:, pl.ds(al(p, 128), 128)])
             col = lax.broadcasted_iota(jnp.int32, (1, KEYS), 1)
             m = meta[c]
             c0 = jnp.concatenate([m[0:1, :]] * (KEYS // 128), axis=1)
             c1 = jnp.concatenate([m[1:2, :]] * (KEYS // 128), axis=1)
             count = jnp.where(col < PATCH, c0, jnp.where(col < PATCH_SLOT, 0.0, c1))
             count = jnp.where(col < PATCH_SLOT + PATCH, count, 0.0)
-            s = jnp.where(count > 0.0, s, NEG_LARGE)
-            e = jnp.exp(s - jnp.max(s, axis=-1, keepdims=True)) * count
-            prob = (e / jnp.sum(e, axis=-1, keepdims=True)).astype(BF)
-            pc[pl.ds(al(i, 2 * TOK), 2 * TOK), :] = prob
-            a2[rows, pl.ds(al(p, 128), 128)] = joined(
-                mm(prob, kv[:, pl.ds(al(p, 128) + D, 128)])
+
+            @pl.loop(0, 6, unroll=3)
+            def _(p):
+                qq = halves(q2[rows, pl.ds(al(p, 128), 128)]) * BF(0.125)
+                s = mm_nt(qq, kv[:, pl.ds(al(p, 128), 128)])
+                s = jnp.where(count > 0.0, s, NEG_LARGE)
+                e = jnp.exp(s - jnp.max(s, axis=-1, keepdims=True)) * count
+                prob = (e * (1.0 / jnp.sum(e, axis=-1, keepdims=True))).astype(BF)
+                pc[pl.ds(al(6 * c + p, 2 * TOK), 2 * TOK), :] = prob
+                a2[rows, pl.ds(al(p, 128), 128)] = joined(
+                    mm(prob, kv[:, pl.ds(al(p, 128) + D, 128)])
+                ).astype(BF)
+
+            sb[rows, :] = (
+                x1[rows, :] + mm(a2[rows, :], wide[:, UO_AT : UO_AT + D]) + vec[V_UO : V_UO + 1, :D]
             ).astype(BF)
-
-        sb[...] = (
-            x1[...] + mm(a2[...], wide[:, UO_AT : UO_AT + D]) + vec[V_UO : V_UO + 1, :D]
-        ).astype(BF)
-        copies["x2"].start()
+            x2_copy(c).start()
+
         copies["old"].start()
 
         h1T[...] = h1[...].T
@@ -930,29 +916,41 @@
         a2T[...] = a2[...].T
         tlT[...] = tl[...].T
 
-        copies["dx2"].wait_recv()
-        t1[...] = mm_nt(rb[...], wide[:, UO_AT : UO_AT + D]).astype(BF)
+        part_at = at1[CROSS_KV]
+
+        def attend_back(c, p, take_keys):
+            rows = pl.ds(c * TOK, TOK)
+            lanes, vlanes = pl.ds(al(p, 128), 128), pl.ds(al(p, 128) + D, 128)
+            qq = halves(q2[rows, lanes]) * BF(0.125)
+            do = halves(t1[rows, lanes])
+            prob = pc[pl.ds(al(6 * c + p, 2 * TOK), 2 * TOK), :]
+            pf = prob.astype(F32)
+            dp = mm_nt(do, kv[:, vlanes])
+            ds = (pf * (dp - jnp.sum(pf * dp, axis=-1, keepdims=True))).astype(BF)
+            am[rows, lanes] = (joined(mm(ds, kv[:, lanes])) * 0.125).astype(BF)
+            take_keys(p, 0, lanes, mm_tn(qq, ds))
+            take_keys(p, 1, vlanes, mm_tn(do, prob))
+
+        def part_rows(p, k, j):
+            return pl.ds(pl.multiple_of(part_at + ((2 * p + k) * 4 + j) * 128, 8), 128)
+
+        def keep(p, k, lanes, term):
+            for j in range(4):
+                gf[part_rows(p, k, j), :] = term[:, 128 * j : 128 * j + 128]
+
+        def complete(p, k, lanes, term):
+            for j in range(4):
+                cols = slice(128 * j, 128 * j + 128)
+                dkvt[lanes, cols] = (gf[part_rows(p, k, j), :] + term[:, cols]).astype(BF)
+
+        for c, take_keys in enumerate((keep, complete)):
+            rows = pl.ds(c * TOK, TOK)
+            dx2_copy(c).wait_recv()
+            t1[rows, :] = mm_nt(rb[rows, :], wide[:, UO_AT : UO_AT + D]).astype(BF)
+            pl.loop(0, 6, unroll=3)(functools.partial(attend_back, c, take_keys=take_keys))
+
         put_vector(at1[CROSS_OUT_BIAS], column_total(rb, slice(None)))
         matrix_grad(at1[CROSS_OUT], 6, a2T, rb)
-
-        @pl.loop(0, 6)
-        def _(p):
-            lanes, vlanes = pl.ds(al(p, 128), 128), pl.ds(al(p, 128) + D, 128)
-            dk = dv = None
-            for c in range(2):
-                rows = pl.ds(c * TOK, TOK)
-                qq = halves(q2[rows, lanes]) * BF(0.125)
-                do = halves(t1[rows, lanes])
-                prob = pc[pl.ds(al(2 * p + c, 2 * TOK), 2 * TOK), :]
-                pf = prob.astype(F32)
-                dp = mm_nt(do, kv[:, vlanes])
-                ds = (pf * (dp - jnp.sum(pf * dp, axis=-1, keepdims=True))).astype(BF)
-                am[rows, lanes] = (joined(mm(ds, kv[:, lanes])) * 0.125).astype(BF)
-                dk_c, dv_c = mm_tn(qq, ds), mm_tn(do, prob)
-                dk, dv = (dk_c, dv_c) if c == 0 else (dk + dk_c, dv + dv_c)
-            dkvt[lanes, :] = dk.astype(BF)
-            dkvt[vlanes, :] = dv.astype(BF)
-
         put_vector(at1[CROSS_QUERY_BIAS], column_total(am, slice(None)))
         matrix_grad(at1[CROSS_QUERY], 6, h2T, am)
         acc[...] = mm_nt(am[...], wide[:, UQ_AT : UQ_AT + D])
@@ -963,7 +961,9 @@
             sb_[rows, :] = full.astype(BF)
 
         sb_ = h2
-        norm_backward(x1, acc, V_G2, write_dx1, at1[NORM_TWO_GAIN], at1[NORM_TWO_SHIFT], gf)
+        gg, gc = norm_backward(x1, acc, V_G2, write_dx1)
+        put_vector(at1[NORM_TWO_GAIN], gg)
+        put_vector(at1[NORM_TWO_SHIFT], gc)
         matrix_grad(at1[CROSS_KV], 12, tlT, dkvt, transposed=True)
         kv[...] = dkvt[...].T
         put_vector(at1[CROSS_VALUE_BIAS], column_total(kv, slice(D, 2 * D)))
@@ -986,9 +986,9 @@
 
         one.add_core()
         one.start_y()
-        give(0, core_peer)
-
-        @pl.loop(0, 12)
+        pl.semaphore_signal(free, inc=1, device_id=core_peer, device_id_type=MESH)
+
+        @pl.loop(0, 12, unroll=4)
         def _(i):
             c, p = i // 6, i % 6
             rows = pl.ds(al(c, TOK), TOK)
@@ -1011,7 +1011,9 @@
         def write_dx0(rows, dv):
             dx[rows, :] = dx[rows, :] + dv
 
-        norm_backward(xin, acc, V_G1, write_dx0, at0[NORM_ONE_GAIN], at0[NORM_ONE_SHIFT], gf)
+        gg, gc = norm_backward(xin, acc, V_G1, write_dx0)
+        put_vector(at0[NORM_ONE_GAIN], gg)
+        put_vector(at0[NORM_ONE_SHIFT], gc)
         dcap[...] = dx[first, :]
         dcap_b[...] = dx[later, :].astype(BF)
         copies["dcap"].start()
@@ -1021,15 +1023,16 @@
         gf[pl.ds(at0[NORM_TWO_GAIN], WINDOW - row0[NORM_TWO_GAIN]), :] = carry[
             row0[NORM_TWO_GAIN] - WINDOW + CARRY :, :
         ]
-        take(0)
+        pl.semaphore_wait(free, 1)
         zero.cast(CARRY)
         zero.add_core()
         rest_of_scatter(one, zero)
-        one.sent()
         copies["out"].wait_recv()
         out[...] = ob[...]
-        for name in ("dy", "x2", "dcap", "dtile"):
+        for name in ("dy", "dcap", "dtile"):
             copies[name].wait_send()
+        for c in range(2):
+            x2_copy(c).wait_send()
         copies["old"].wait()
         square_sums()
 
@@ -1061,34 +1064,44 @@
             for j in range(6):
                 gf[pl.ds(al(6 * b + j, 256), 256), :] = dg[:, 128 * j : 128 * j + 128]
 
-        copies["x2"].wait_recv()
-        norm_forward(rb, h1, V_G3, V_C3)
-        acc[...] = jnp.zeros_like(acc)
-
-        @pl.loop(0, 4)
-        def _(b):
-            cols = pl.ds(al(b, D), D)
-            x1[...] = mm(h1[...], wide[:, cols]) + vec[V_B1 : V_B1 + 1, cols]
-
-            @pl.loop(0, 8)
-            def _(i):
-                rows = pl.ds(al(i, 32), 32)
-                for j in range(6):
-                    z = x1[rows, 128 * j : 128 * j + 128]
-                    phi = 0.5 + 0.5 * lax.erf(z * np.float32(np.sqrt(0.5)))
-                    dens = jnp.exp(-0.5 * z * z) * np.float32(1.0 / np.sqrt(2.0 * np.pi))
-                    lanes = pl.ds(al(b, D) + 128 * j, 128)
-                    big1[rows, lanes] = (z * phi).astype(BF)
-                    dg = gf[pl.ds(al(6 * b + j, 256) + al(i, 32), 32), :]
-                    big2[rows, lanes] = (dg * (phi + z * dens)).astype(BF)
-
-            acc[...] = acc[...] + mm_nt(big2[:, cols], wide[:, cols])
-
         def write_dx2(rows, dv):
             sb[rows, :] = (dy[rows, :].astype(F32) + dv).astype(BF)
 
-        norm_backward(rb, acc, V_G3, write_dx2, 12, 18, pfx)
-        copies["dx2"].start()
+        vec[V_SUMS : V_SUMS + 2, :] = jnp.zeros((2, FF), F32)
+
+        @pl.loop(0, 2)
+        def _(c):
+            cap_rows = pl.ds(al(c, TOK), TOK)
+            x2_copy(c).wait_recv()
+            norm_forward(rb, h1, V_G3, V_C3, c * TOK, TOK)
+            acc[cap_rows, :] = jnp.zeros((TOK, D), F32)
+
+            @pl.loop(0, 4)
+            def _(b):
+                cols = pl.ds(al(b, D), D)
+                x1[0:TOK, :] = mm(h1[cap_rows, :], wide[:, cols]) + vec[V_B1 : V_B1 + 1, cols]
+
+                @pl.loop(0, 4)
+                def _(i):
+                    rows = pl.ds(al(c, TOK) + al(i, 32), 32)
+                    for j in range(6):
+                        z = x1[pl.ds(al(i, 32), 32), 128 * j : 128 * j + 128]
+                        phi = 0.5 + 0.5 * lax.erf(z * np.float32(np.sqrt(0.5)))
+                        dens = jnp.exp(-0.5 * z * z) * np.float32(1.0 / np.sqrt(2.0 * np.pi))
+                        lanes = pl.ds(al(b, D) + 128 * j, 128)
+                        big1[rows, lanes] = (z * phi).astype(BF)
+                        dg = gf[pl.ds(al(6 * b + j, 256) + al(c, TOK) + al(i, 32), 32), :]
+                        big2[rows, lanes] = (dg * (phi + z * dens)).astype(BF)
+
+                acc[cap_rows, :] = acc[cap_rows, :] + mm_nt(big2[cap_rows, cols], wide[:, cols])
+
+            gg, gc = norm_backward(rb, acc, V_G3, write_dx2, c * TOK, TOK)
+            vec[V_SUMS : V_SUMS + 1, :D] = vec[V_SUMS : V_SUMS + 1, :D] + gg
+            vec[V_SUMS + 1 : V_SUMS + 2, :D] = vec[V_SUMS + 1 : V_SUMS + 2, :D] + gc
+            dx2_copy(c).start()
+
+        put_vector(12, vec[V_SUMS : V_SUMS + 1, :D], pfx)
+        put_vector(18, vec[V_SUMS + 1 : V_SUMS + 2, :D], pfx)
 
         h1T[...] = h1[...].T
         pfx[0:12, :] = jnp.zeros((12, 128), F32)
@@ -1125,19 +1138,20 @@
         matrix_grad(at0[MLP_UP], 24, h1T, big2)
         one.add_core()
         one.start_y()
-        give(0, core_peer)
+        pl.semaphore_signal(free, inc=1, device_id=core_peer, device_id_type=MESH)
         gf[pl.ds(at0[MLP_DOWN], CARRY), :] = carry[...]
-        take(0)
+        pl.semaphore_wait(free, 1)
         zero.cast(CARRY)
         zero.add_core()
         rest_of_scatter(one, zero)
-        one.sent()
         copies["dtile"].wait_recv()
         dtile[...] = dtile_b[0:PATCH, :].astype(F32)
         copies["dcap"].wait_recv()
         dcap[...] = dcap_b[...].astype(F32)
-        for name in ("cap", "tile", "meta", "dx2", "pfx", "out"):
+        for name in ("cap", "tile", "meta", "pfx", "out"):
             copies[name].wait_send()
+        for c in range(2):
+            dx2_copy(c).wait_send()
         copies["old"].wait()
         square_sums()
 
@@ -1178,12 +1192,12 @@
             *[fl(both, D) for _ in range(3)],
             fl(16, FF), fl(2, 8, 128), bf(TOK, D), fl(LEAD, 128), fl(LEAD, 128), fl(CARRY, 128),
             bf(TOK, D), bf(PATCH_SENT, D),
-            bf(PIECES, 4 * PIECE, 128), bf(PIECES, 2 * PIECE, 128), bf(PIECES, PIECE, 128),
-            bf(PIECES, 2, PIECE, 128), bf(PIECES, 2, PIECE, 128), fl(2432, 128), fl(10, SEGS, 128),
-            dma((5,)), dma, dma((12,)), dma((12,)),
-            *[dma((PIECES,)) for _ in range(6)],
-            *[dma((PIECES, 2)) for _ in range(4)],
-            pltpu.SemaphoreType.REGULAR((5,)), dma((6,)), dma((6,)),
+            bf(PIECES, 4 * PIECE, 128), bf(2, PIECES, 2 * PIECE, 128), bf(2, PIECES, PIECE, 128),
+            bf(2, PIECES, 2, PIECE, 128), bf(2, PIECES, 2, PIECE, 128), fl(2432, 128), fl(10, SEGS, 128),
+            dma((5,)), dma, dma((16,)), dma((16,)),
+            *[dma((2, PIECES)) for _ in range(6)],
+            *[dma((2, PIECES, 2)) for _ in range(4)],
+            pltpu.SemaphoreType.REGULAR, dma((6,)), dma((6,)),
         ],
         compiler_params=pltpu.CompilerParams(
             collective_id=0, has_side_effects=True, vmem_limit_bytes=63 * 2**20

time: 210 us -> 170 us (0.81)
  Pallas kernels: 196 us -> 156 us
    pallas_call x1, Pallas kernels: 196 us -> 156 us  [pair_call(): pl.pallas_call(pair_kernel, in_specs=[vm, vm, vm, sm, sm, sm, hbm], out_s...]
where the time goes in v1:
time: 170 us
  Pallas kernels  156 us (92%)
  other arithmetic  6.73 us (4%)
  local copies, waits for them, and re-layouts  3.9 us (2%)
  between operations  3.26 us (2%)
    pallas_call x1, Pallas kernels, pair_call(): pl.pallas_call(pair_kernel, in_specs=[vm, vm, vm, sm, sm, sm, hbm], out_s...  156 us
    mul x1, other arithmetic, adam_step(): -LEARN_RATE  4.54 us
    unnamed x14, local copies, waits for them, and re-layouts  3.9 us

profile of v1, /device:TPU:0, one launch (start us, length us, event | category | flops | bytes accessed | tf_op | source)
XLA Modules:
  0.0 169.6 jit_solution(14807930519038662422)
XLA Ops:
  0.7 0.8 and_reduce_fusion
  2.2 0.0 copy-start.4
  2.2 155.7 %shard_map.196 = (f32[2312,128]{1,0:T(8,128)}, f32[24,128]{1,0:T(8,128)}, bf16[2320,128]{1,0:T(8,128)(2,1)}, bf16[128,768]{1,0:T(8,128)(2,1)}, f32[128,768]{1,0:T(8,128)}, /*index=5*/f32[196,768]{1,0:T(8,128)}) custom-call(bf16[128,768]{1,0:T(8,128)(2,1)} %bitcast.10, bf16[196,768]{1,0:T(8,128)(2,1)} %bitcast.8, bf16[128,768]{1,0:T(8,128)(2,1)} %bitcast.11, ...), custom_call_target="tpu_custom_call" | custom-call | tf_op jit(solution)/shard_map/pallas_call | solution.py:1175
  157.9 0.0 copy-done.4
  157.9 1.3 sqrt_reduce_fusion
  160.0 0.0 copy-start.1
  160.0 4.5 %add_multiply_fusion = (f32[2312,128]{1,0:T(8,128)}, f32[2312,128]{1,0:T(8,128)}, f32[2312,128]{1,0:T(8,128)}) fusion(bf16[2320,128]{1,0:T(8,128)(2,1)} %get-tuple-element.20, s32[]{:T(128)S(6)} %select_n.33, bf16[36992,128]{1,0:T(8,128)(2,1)} %weights.1, s32[]{:T(128)S(6)} %select_n.32, pred[2312]{0:T(1024)(128)(4,1)S(1)} %and_reduce_fusion, pred[]{:T(512)S(6)} %eq.5, ...), kind=kLoop, calls=%fused_computation.2 | loop fusion | flops 5326848 | bytes 8288533 | tf_op jit(solution)/shard_map/mul | solution.py:195
  164.5 0.0 copy-start.3
  164.5 0.0 copy-start.2
  164.5 0.0 copy-done.1
  164.6 0.0 copy-start
  164.6 1.4 copy.24
  166.0 0.0 copy-done.3
  166.0 0.7 copy.29
  166.7 0.0 copy-done.2
  166.7 0.7 copy.30
  167.4 0.0 copy-done
  167.4 1.0 copy.31
  (1 shorter events, 0.0 us)
Async XLA Ops:
  2.2 155.7 %copy-start.4 = (f32[21,1]{1,0:T(8,128)S(1)}, f32[21,1]{1,0:T(8,128)}, u32[]{:S(2)}) copy-start(f32[21,1]{1,0:T(8,128)} %constant.96) | copy-start | bytes 256
  160.0 4.6 %copy-start.1 = (f32[196,768]{1,0:T(8,128)S(1)}, f32[196,768]{1,0:T(8,128)}, u32[]{:S(2)}) copy-start(f32[196,768]{1,0:T(8,128)} %get-tuple-element.17) | copy-start | bytes 1806340
  164.5 1.5 copy-start.3
  164.5 2.1 %copy-start.2 = (f32[128,768]{1,0:T(8,128)S(1)}, f32[128,768]{1,0:T(8,128)}, u32[]{:S(2)}) copy-start(f32[128,768]{1,0:T(8,128)} %get-tuple-element.16) | copy-start | bytes 1179652
  164.6 2.9 %copy-start = (f32[2312,128]{1,0:T(8,128)S(1)}, f32[2312,128]{1,0:T(8,128)}, u32[]{:S(2)}) copy-start(f32[2312,128]{1,0:T(8,128)} %get-tuple-element.65) | copy-start | bytes 3551236

commit v2 on v1

--- a/solution.py
+++ b/solution.py
@@ -443,6 +443,7 @@
 BF, F32 = jnp.bfloat16, jnp.float32
 MESH = pl.DeviceIdType.MESH
 SHARD, PIECES, PIECE = 2312, 5, 464
+OLD = 2320
 PADDED = PIECES * PIECE
 WINDOW = 8 * SHARD
 CARRY = 96
@@ -518,6 +519,12 @@
     x_peer = {DP: me, FSDP: other}
     up_peer = at_dp(jnp.minimum(my_z + 1, NZ - 1), my_y, my_core)
     down_peer = at_dp(jnp.maximum(my_z - 1, 0), my_y, my_core)
+    barrier = pltpu.get_barrier_semaphore()
+    for peer in (core_peer, y_peer, x_peer):
+        pl.semaphore_signal(barrier, inc=1, device_id=peer, device_id_type=MESH)
+    for step in range(1, NZ):
+        peer = at_dp((my_z + step) % NZ, my_y, my_core)
+        pl.semaphore_signal(barrier, inc=1, device_id=peer, device_id_type=MESH)
     row0 = row_starts()
 
     cuts = [0, 13856, 18480, 23088, 32320, weights.shape[0]]
@@ -548,7 +555,7 @@
         out=to_other(t1.at[first], ob, 7),
         pfx=to_other(pfx, pfx_in, 8),
         old=to_other(
-            weights.at[pl.ds(pl.multiple_of(((2 * me + other) % 16) * SHARD - 8 * other, 16), PADDED)], old_out, 9
+            weights.at[pl.ds(pl.multiple_of(((2 * me + other) % 16) * SHARD - 8 * other, 16), OLD)], old_out, 9
         ),
         dcap=to_other(dcap_b, dcap_b, 10),
         dtile=to_other(dtile_b, dtile_b, 11),
@@ -564,7 +571,9 @@
     def dx2_copy(c):
         return to_other_half(c, 14)
 
-    tl[...] = jnp.zeros_like(tl)
+    after = PATCH_SLOT + PATCH_SENT
+    tl[0:PATCH_SLOT, :] = jnp.zeros((PATCH_SLOT, D), BF)
+    tl[after:, :] = jnp.zeros((KEYS - after, D), BF)
     tl[0:PATCH, :] = tiles[...]
     counts = []
     for g in range(2):
@@ -578,13 +587,8 @@
         rows8 == 0, counts[0], jnp.where(rows8 == 1, counts[1], length[0])
     ).astype(F32)
 
-    barrier = pltpu.get_barrier_semaphore()
-    for peer in (core_peer, y_peer, x_peer):
-        pl.semaphore_signal(barrier, inc=1, device_id=peer, device_id_type=MESH)
-    for step in range(1, NZ):
-        peer = at_dp((my_z + step) % NZ, my_y, my_core)
-        pl.semaphore_signal(barrier, inc=1, device_id=peer, device_id_type=MESH)
-    pl.semaphore_wait(barrier, 3 + NZ - 1)
+    def all_here():
+        pl.semaphore_wait(barrier, 3 + NZ - 1)
 
     def vector(row, at, n, col=0):
         block = fw[pl.ds(at, n // 128), :].astype(F32)
@@ -627,7 +631,7 @@
         return jnp.sum(ref[:, cols].astype(F32), axis=0, keepdims=True)
 
     def matrix_grad(at, k, lhs_t, rhs, transposed=False):
-        @pl.loop(0, k // 2)
+        @pl.loop(0, k // 2, unroll=3)
         def _(m):
             cols = pl.ds(al(m, 256), 256)
             res = mm_nt(lhs_t[...], rhs[cols, :]) if transposed else mm(lhs_t[...], rhs[:, cols])
@@ -688,10 +692,6 @@
                 self.core(s).wait_recv()
                 rows = pl.ds(slot(self.w, s, my_core), 4 * PIECE)
                 fw[rows, :] = fw[rows, :] + from_core[s]
-
-        def start_y(self):
-            @pl.loop(0, PIECES)
-            def _(s):
                 self.y(s).start()
 
         def add_y(self, s):
@@ -709,21 +709,21 @@
                 if goal < NZ - 1:
                     pl.when(my_z == NZ - 1)(self.down(s, h).start)
 
-        def relay(self, s):
+        def relay(self, s, hop):
             for h in range(2):
                 goal = 2 * h + self.w
                 mine = self.held(s, h)
-                if goal > 1:
-
-                    @pl.when((my_z > 0) & (my_z < goal))
+                if hop < goal:
+
+                    @pl.when(my_z == hop)
                     def _():
                         self.up(s, h).wait_recv()
                         mine[...] = mine[...] + from_low[self.w, s, h]
                         self.up(s, h).start()
 
-                if goal < NZ - 2:
-
-                    @pl.when((my_z < NZ - 1) & (my_z > goal))
+                if NZ - 1 - hop > goal:
+
+                    @pl.when(my_z == NZ - 1 - hop)
                     def _():
                         self.down(s, h).wait_recv()
                         mine[...] = mine[...] + from_high[self.w, s, h]
@@ -756,18 +756,18 @@
                     pl.when(my_z > goal)(self.down(s, h).wait_send)
 
     def rest_of_scatter(one, zero):
-        zero.start_y()
         pl.loop(0, PIECES)(one.add_y)
         pl.loop(0, PIECES)(one.from_ends)
 
-        @pl.loop(0, PIECES)
-        def _(s):
-            zero.add_y(s)
-            one.relay(s)
-            pl.when(s > 0)(lambda: zero.from_ends(s - 1))
-
-        zero.from_ends(PIECES - 1)
-        pl.loop(0, PIECES)(zero.relay)
+        def step(s, when):
+            when(s < PIECES, lambda: zero.add_y(s))
+            when(s < PIECES, lambda: one.relay(s, 1))
+            when((s > 0) & (s <= PIECES), lambda: one.relay(s - 1, 2))
+            when((s > 0) & (s <= PIECES), lambda: zero.from_ends(s - 1))
+            when((s > 1) & (s <= PIECES + 1), lambda: zero.relay(s - 2, 1))
+            when((s > 2) & (s <= PIECES + 2), lambda: zero.relay(s - 3, 2))
+
+        pl.loop(0, PIECES + 3)(lambda s: step(s, lambda is_so, do: pl.when(is_so)(do)))
         pl.loop(0, PIECES)(one.collect)
         pl.loop(0, PIECES)(zero.collect)
         one.sent()
@@ -819,7 +819,6 @@
         at1 = {k: CARRY - WINDOW + v for k, v in row0.items()}
         one, zero = Scatter(1, 0), Scatter(0, 0)
         xin[first, :] = cap[...]
-        copies["dy"].start()
         loads[0].wait()
         vector(V_G1, at[NORM_ONE_GAIN], D)
         vector(V_C1, at[NORM_ONE_SHIFT], D)
@@ -830,7 +829,6 @@
         widen(at[SELF_QKV], 18, QKV_AT)
         for c in loads[1:]:
             c.wait()
-        copies["lead"].start()
         vector(V_BO, at[SELF_OUT_BIAS], D)
         vector(V_G2, at[NORM_TWO_GAIN], D)
         vector(V_C2, at[NORM_TWO_SHIFT], D)
@@ -841,13 +839,15 @@
         widen(at[CROSS_QUERY], 6, UQ_AT)
         widen(at[CROSS_KV], 12, UKV_AT)
         widen(at[CROSS_OUT], 6, UO_AT)
+        all_here()
+        copies["dy"].start()
+        copies["lead"].start()
 
         copies["cap"].wait_recv()
         norm_forward(xin, h1, V_G1, V_C1)
 
-        @pl.loop(0, 3)
-        def _(j):
-            cols = pl.ds(al(j, D), D)
+        for j in range(3):
+            cols = slice(D * j, D * j + D)
             big1[:, cols] = (mm(h1[...], wide[:, cols]) + vec[V_BQKV : V_BQKV + 1, cols]).astype(BF)
 
         copies["meta"].wait_recv()
@@ -874,11 +874,10 @@
         q2[...] = (mm(h2[...], wide[:, UQ_AT : UQ_AT + D]) + vec[V_UQ : V_UQ + 1, :D]).astype(BF)
         copies["tile"].wait_recv()
 
-        @pl.loop(0, 2)
-        def _(j):
-            cols = pl.ds(al(j, D), D)
+        for j in range(2):
+            cols = slice(D * j, D * j + D)
             kv[:, cols] = (
-                mm(tl[...], wide[:, pl.ds(al(j, D) + UKV_AT, D)]) + vec[V_BKV : V_BKV + 1, cols]
+                mm(tl[...], wide[:, UKV_AT + D * j : UKV_AT + D * j + D]) + vec[V_BKV : V_BKV + 1, cols]
             ).astype(BF)
 
         @pl.loop(0, 2)
@@ -953,40 +952,37 @@
         matrix_grad(at1[CROSS_OUT], 6, a2T, rb)
         put_vector(at1[CROSS_QUERY_BIAS], column_total(am, slice(None)))
         matrix_grad(at1[CROSS_QUERY], 6, h2T, am)
-        acc[...] = mm_nt(am[...], wide[:, UQ_AT : UQ_AT + D])
-
-        def write_dx1(rows, dv):
-            full = rb[rows, :].astype(F32) + dv
-            dx[rows, :] = full
-            sb_[rows, :] = full.astype(BF)
-
-        sb_ = h2
-        gg, gc = norm_backward(x1, acc, V_G2, write_dx1)
-        put_vector(at1[NORM_TWO_GAIN], gg)
-        put_vector(at1[NORM_TWO_SHIFT], gc)
         matrix_grad(at1[CROSS_KV], 12, tlT, dkvt, transposed=True)
         kv[...] = dkvt[...].T
         put_vector(at1[CROSS_VALUE_BIAS], column_total(kv, slice(D, 2 * D)))
-
-        def tile_grad(rows):
-            keys = mm_nt(kv[rows, 0:D], wide[:, UKV_AT : UKV_AT + D])
-            return keys + mm_nt(kv[rows, D : 2 * D], wide[:, UKV_AT + D : UKV_AT + 2 * D])
-
-        dtile[...] = tile_grad(pl.ds(0, PATCH_SENT))[:PATCH]
-        dtile_b[...] = tile_grad(pl.ds(PATCH_SLOT, PATCH_SENT)).astype(BF)
-        copies["dtile"].start()
         copies["pfx"].wait_recv()
         gf[pl.ds(at1[NORM_THREE_GAIN], LEAD - 12), :] = pfx_in[12:, :]
         copies["lead"].wait_send()
         one.cast(CARRY)
         carry[...] = gf[0:CARRY, :]
-        put_vector(at0[SELF_OUT_BIAS], column_total(sb_, slice(None)))
-        matrix_grad(at0[SELF_OUT], 6, amT, sb_)
-        t1[...] = mm_nt(sb_[...], wide[:, WO_AT : WO_AT + D]).astype(BF)
-
+
+        def tile_grad(rows):
+            return mm_nt(kv[rows, :], wide[:, UKV_AT : UKV_AT + 2 * D])
+
+        dtile[...] = tile_grad(pl.ds(0, PATCH_SENT))[:PATCH]
+        dtile_b[...] = tile_grad(pl.ds(PATCH_SLOT, PATCH_SENT)).astype(BF)
+        copies["dtile"].start()
         one.add_core()
-        one.start_y()
         pl.semaphore_signal(free, inc=1, device_id=core_peer, device_id_type=MESH)
+        acc[...] = mm_nt(am[...], wide[:, UQ_AT : UQ_AT + D])
+        e1 = h2
+
+        def write_dx1(rows, dv):
+            full = rb[rows, :].astype(F32) + dv
+            dx[rows, :] = full
+            e1[rows, :] = full.astype(BF)
+
+        gg, gc = norm_backward(x1, acc, V_G2, write_dx1)
+        put_vector(at0[NORM_TWO_GAIN], gg)
+        put_vector(at0[NORM_TWO_SHIFT], gc)
+        put_vector(at0[SELF_OUT_BIAS], column_total(e1, slice(None)))
+        matrix_grad(at0[SELF_OUT], 6, amT, e1)
+        t1[...] = mm_nt(e1[...], wide[:, WO_AT : WO_AT + D]).astype(BF)
 
         @pl.loop(0, 12, unroll=4)
         def _(i):
@@ -1004,9 +1000,7 @@
             big2[rows, klanes] = mm_tn(ds, qq).astype(BF)
             big2[rows, vlanes] = mm_tn(prob, do).astype(BF)
 
-        for j in range(3):
-            part = mm_nt(big2[:, D * j : D * j + D], wide[:, D * j : D * j + D])
-            acc[...] = part if j == 0 else acc[...] + part
+        acc[...] = mm_nt(big2[:, : 3 * D], wide[:, : 3 * D])
 
         def write_dx0(rows, dv):
             dx[rows, :] = dx[rows, :] + dv
@@ -1020,8 +1014,8 @@
         put_vector(at0[SELF_QUERY_BIAS], column_total(big2, slice(0, D)))
         put_vector(at0[SELF_VALUE_BIAS], column_total(big2, slice(2 * D, 3 * D)))
         matrix_grad(at0[SELF_QKV], 18, h1T, big2)
-        gf[pl.ds(at0[NORM_TWO_GAIN], WINDOW - row0[NORM_TWO_GAIN]), :] = carry[
-            row0[NORM_TWO_GAIN] - WINDOW + CARRY :, :
+        gf[pl.ds(at0[CROSS_QUERY], WINDOW - row0[CROSS_QUERY]), :] = carry[
+            row0[CROSS_QUERY] - WINDOW + CARRY :, :
         ]
         pl.semaphore_wait(free, 1)
         zero.cast(CARRY)
@@ -1037,9 +1031,11 @@
         square_sums()
 
     def mlp_role():
+        all_here()
+        copies["meta"].start()
         copies["cap"].start()
+        copies["cap"].wait_send()
         copies["tile"].start()
-        copies["meta"].start()
         base = LEAD - weights.shape[0]
         at = {k: base + v for k, v in row0.items()}
         at0 = {k: CARRY - weights.shape[0] + v for k, v in row0.items()}
@@ -1074,27 +1070,25 @@
             cap_rows = pl.ds(al(c, TOK), TOK)
             x2_copy(c).wait_recv()
             norm_forward(rb, h1, V_G3, V_C3, c * TOK, TOK)
-            acc[cap_rows, :] = jnp.zeros((TOK, D), F32)
+            z_parts = [x1.at[first], x1.at[later], dx.at[first], dx.at[later]]
+            for b in range(4):
+                cols = slice(D * b, D * b + D)
+                z_parts[b][...] = mm(h1[cap_rows, :], wide[:, cols]) + vec[V_B1 : V_B1 + 1, cols]
 
             @pl.loop(0, 4)
-            def _(b):
-                cols = pl.ds(al(b, D), D)
-                x1[0:TOK, :] = mm(h1[cap_rows, :], wide[:, cols]) + vec[V_B1 : V_B1 + 1, cols]
-
-                @pl.loop(0, 4)
-                def _(i):
-                    rows = pl.ds(al(c, TOK) + al(i, 32), 32)
-                    for j in range(6):
-                        z = x1[pl.ds(al(i, 32), 32), 128 * j : 128 * j + 128]
-                        phi = 0.5 + 0.5 * lax.erf(z * np.float32(np.sqrt(0.5)))
-                        dens = jnp.exp(-0.5 * z * z) * np.float32(1.0 / np.sqrt(2.0 * np.pi))
-                        lanes = pl.ds(al(b, D) + 128 * j, 128)
-                        big1[rows, lanes] = (z * phi).astype(BF)
-                        dg = gf[pl.ds(al(6 * b + j, 256) + al(c, TOK) + al(i, 32), 32), :]
-                        big2[rows, lanes] = (dg * (phi + z * dens)).astype(BF)
-
-                acc[cap_rows, :] = acc[cap_rows, :] + mm_nt(big2[cap_rows, cols], wide[:, cols])
-
+            def _(i):
+                here = pl.ds(al(i, 32), 32)
+                rows = pl.ds(al(c, TOK) + al(i, 32), 32)
+                for k in range(24):
+                    z = z_parts[k // 6][here, 128 * (k % 6) : 128 * (k % 6) + 128]
+                    phi = 0.5 + 0.5 * lax.erf(z * np.float32(np.sqrt(0.5)))
+                    dens = jnp.exp(-0.5 * z * z) * np.float32(1.0 / np.sqrt(2.0 * np.pi))
+                    lanes = slice(128 * k, 128 * k + 128)
+                    big1[rows, lanes] = (z * phi).astype(BF)
+                    dg = gf[pl.ds(256 * k + al(c, TOK) + al(i, 32), 32), :]
+                    big2[rows, lanes] = (dg * (phi + z * dens)).astype(BF)
+
+            acc[cap_rows, :] = mm_nt(big2[cap_rows, :], wide[:, W1_AT : W1_AT + FF])
             gg, gc = norm_backward(rb, acc, V_G3, write_dx2, c * TOK, TOK)
             vec[V_SUMS : V_SUMS + 1, :D] = vec[V_SUMS : V_SUMS + 1, :D] + gg
             vec[V_SUMS + 1 : V_SUMS + 2, :D] = vec[V_SUMS + 1 : V_SUMS + 2, :D] + gc
@@ -1116,12 +1110,10 @@
         copies["old"].start()
 
         acc[...] = rb[...].astype(F32) + vec[V_B2 : V_B2 + 1, :D]
-
-        @pl.loop(0, 4)
-        def _(b):
-            cols = pl.ds(al(b, D), D)
-            acc[...] = acc[...] + mm(big1[:, cols], wide[:, pl.ds(al(b, D) + W2_AT, D)])
-            pc[pl.ds(al(b, D), D), 0:256] = big1[:, cols].T
+        for b in range(4):
+            cols = slice(D * b, D * b + D)
+            acc[...] = acc[...] + mm(big1[:, cols], wide[:, W2_AT + D * b : W2_AT + D * b + D])
+            pc[D * b : D * b + D, 0:256] = big1[:, cols].T
 
         t1[first, :] = acc[first, :].astype(BF)
         copies["out"].start()
@@ -1137,7 +1129,6 @@
         put_vector(at0[MLP_UP_BIAS], column_total(big2, slice(None)))
         matrix_grad(at0[MLP_UP], 24, h1T, big2)
         one.add_core()
-        one.start_y()
         pl.semaphore_signal(free, inc=1, device_id=core_peer, device_id_type=MESH)
         gf[pl.ds(at0[MLP_DOWN], CARRY), :] = carry[...]
         pl.semaphore_wait(free, 1)
@@ -1148,7 +1139,7 @@
         dtile[...] = dtile_b[0:PATCH, :].astype(F32)
         copies["dcap"].wait_recv()
         dcap[...] = dcap_b[...].astype(F32)
-        for name in ("cap", "tile", "meta", "pfx", "out"):
+        for name in ("tile", "meta", "pfx", "out"):
             copies[name].wait_send()
         for c in range(2):
             dx2_copy(c).wait_send()
@@ -1179,13 +1170,13 @@
         out_shape=[
             S((SHARD, 128), F32),
             S((SEGS, 128), F32),
-            S((PADDED, 128), BF),
+            S((OLD, 128), BF),
             S((TOK, D), BF),
             S((TOK, D), F32),
             S((PATCH, D), F32),
         ],
         scratch_shapes=[
-            bf(16 * PADDED, 128), bf(D, WIDE), fl(CARRY + WINDOW + 8, 128), bf(12 * both, KEYS),
+            bf(16 * PADDED, 128), bf(D, WIDE), fl(CARRY + 7 * SHARD + PADDED, 128), bf(12 * both, KEYS),
             bf(12, both, 128), bf(both, FF), bf(both, FF), bf(KEYS, 2 * D), bf(2 * D, KEYS), bf(KEYS, D), bf(D, KEYS),
             *[bf(both, D) for _ in range(10)],
             *[bf(D, both) for _ in range(4)],

time: 170 us -> 157 us (0.924)
  Pallas kernels: 156 us -> 143 us
    pallas_call x1, Pallas kernels: 156 us -> 143 us  [pair_call(): pl.pallas_call(pair_kernel, in_specs=[vm, vm, vm, sm, sm, sm, hbm], out_s...]
where the time goes in v2:
time: 157 us
  Pallas kernels  143 us (91%)
  other arithmetic  6.73 us (4%)
  local copies, waits for them, and re-layouts  3.9 us (2%)
  between operations  3.26 us (2%)
    pallas_call x1, Pallas kernels, pair_call(): pl.pallas_call(pair_kernel, in_specs=[vm, vm, vm, sm, sm, sm, hbm], out_s...  143 us
    mul x1, other arithmetic, adam_step(): -LEARN_RATE  4.54 us
    unnamed x14, local copies, waits for them, and re-layouts  3.9 us

profile of v2, /device:TPU:0, one launch (start us, length us, event | category | flops | bytes accessed | tf_op | source)
XLA Modules:
  0.0 157.2 jit_solution(18390982166352155372)
XLA Ops:
  0.7 0.8 and_reduce_fusion
  2.2 0.0 copy-start.4
  2.2 143.3 %shard_map.196 = (f32[2312,128]{1,0:T(8,128)}, f32[24,128]{1,0:T(8,128)}, bf16[2320,128]{1,0:T(8,128)(2,1)}, bf16[128,768]{1,0:T(8,128)(2,1)}, f32[128,768]{1,0:T(8,128)}, /*index=5*/f32[196,768]{1,0:T(8,128)}) custom-call(bf16[128,768]{1,0:T(8,128)(2,1)} %bitcast.10, bf16[196,768]{1,0:T(8,128)(2,1)} %bitcast.8, bf16[128,768]{1,0:T(8,128)(2,1)} %bitcast.11, ...), custom_call_target="tpu_custom_call" | custom-call | tf_op jit(solution)/shard_map/pallas_call | solution.py:1166
  145.5 0.0 copy-done.4
  145.5 1.3 sqrt_reduce_fusion
  147.6 0.0 copy-start.1
  147.6 4.5 %add_multiply_fusion = (f32[2312,128]{1,0:T(8,128)}, f32[2312,128]{1,0:T(8,128)}, f32[2312,128]{1,0:T(8,128)}) fusion(bf16[2320,128]{1,0:T(8,128)(2,1)} %get-tuple-element.20, s32[]{:T(128)S(6)} %select_n.33, bf16[36992,128]{1,0:T(8,128)(2,1)} %weights.1, s32[]{:T(128)S(6)} %select_n.32, pred[2312]{0:T(1024)(128)(4,1)S(1)} %and_reduce_fusion, pred[]{:T(512)S(6)} %eq.5, ...), kind=kLoop, calls=%fused_computation.2 | loop fusion | flops 5326848 | bytes 8288533 | tf_op jit(solution)/shard_map/mul | solution.py:195
  152.1 0.0 copy-start.3
  152.1 0.0 copy-start.2
  152.1 0.0 copy-done.1
  152.1 0.0 copy-start
  152.2 1.4 copy.24
  153.6 0.0 copy-done.3
  153.6 0.7 copy.29
  154.3 0.0 copy-done.2
  154.3 0.7 copy.30
  155.0 0.0 copy-done
  155.0 1.0 copy.31
  (1 shorter events, 0.0 us)
Async XLA Ops:
  2.2 143.3 %copy-start.4 = (f32[21,1]{1,0:T(8,128)S(1)}, f32[21,1]{1,0:T(8,128)}, u32[]{:S(2)}) copy-start(f32[21,1]{1,0:T(8,128)} %constant.96) | copy-start | bytes 256
  147.6 4.6 %copy-start.1 = (f32[196,768]{1,0:T(8,128)S(1)}, f32[196,768]{1,0:T(8,128)}, u32[]{:S(2)}) copy-start(f32[196,768]{1,0:T(8,128)} %get-tuple-element.17) | copy-start | bytes 1806340
  152.1 1.5 copy-start.3
  152.1 2.1 %copy-start.2 = (f32[128,768]{1,0:T(8,128)S(1)}, f32[128,768]{1,0:T(8,128)}, u32[]{:S(2)}) copy-start(f32[128,768]{1,0:T(8,128)} %get-tuple-element.16) | copy-start | bytes 1179652
  152.1 2.9 %copy-start = (f32[2312,128]{1,0:T(8,128)S(1)}, f32[2312,128]{1,0:T(8,128)}, u32[]{:S(2)}) copy-start(f32[2312,128]{1,0:T(8,128)} %get-tuple-element.65) | copy-start | bytes 3551236

commit v3 on v2

--- a/solution.py
+++ b/solution.py
@@ -600,7 +600,7 @@
             wide[:, col + 128 * j : col + 128 * j + 128] = fw[pl.ds(at + j, rows, stride=k), :]
 
     def norm_forward(src, dst, g, c, at=0, n=2 * TOK):
-        @pl.loop(0, n // 64)
+        @pl.loop(0, n // 64, unroll=2)
         def _(i):
             rows = pl.ds(pl.multiple_of(at + 64 * i, 64), 64)
             v, _ = normed(src[rows, :].astype(F32))
@@ -621,7 +621,7 @@
                 sums[1] + jnp.sum(d, axis=0, keepdims=True),
             )
 
-        return lax.fori_loop(0, n // 64, step, (jnp.zeros((1, D), F32), jnp.zeros((1, D), F32)))
+        return lax.fori_loop(0, n // 64, step, (jnp.zeros((1, D), F32), jnp.zeros((1, D), F32)), unroll=2)
 
     def put_vector(at, row, into=gf):
         for j in range(row.shape[1] // 128):
@@ -700,34 +700,52 @@
             fw[rows, :] = fw[rows, :] + from_y[self.w, s]
             self.over(s).start()
 
-        def from_ends(self, s):
-            self.over(s).wait_recv()
-            for h in range(2):
-                goal = 2 * h + self.w
-                if goal > 0:
-                    pl.when(my_z == 0)(self.up(s, h).start)
-                if goal < NZ - 1:
-                    pl.when(my_z == NZ - 1)(self.down(s, h).start)
-
-        def relay(self, s, hop):
-            for h in range(2):
-                goal = 2 * h + self.w
-                mine = self.held(s, h)
-                if hop < goal:
-
-                    @pl.when(my_z == hop)
-                    def _():
-                        self.up(s, h).wait_recv()
-                        mine[...] = mine[...] + from_low[self.w, s, h]
-                        self.up(s, h).start()
-
-                if NZ - 1 - hop > goal:
-
-                    @pl.when(my_z == NZ - 1 - hop)
-                    def _():
-                        self.down(s, h).wait_recv()
-                        mine[...] = mine[...] + from_high[self.w, s, h]
-                        self.down(s, h).start()
+        def from_ends(self, s, h):
+            if h != self.x:
+                self.over(s).wait_recv()
+            goal = 2 * h + self.w
+            if goal > 0:
+                pl.when(my_z == 0)(self.up(s, h).start)
+            if goal < NZ - 1:
+                pl.when(my_z == NZ - 1)(self.down(s, h).start)
+
+        def relay(self, s, hop, h):
+            goal = 2 * h + self.w
+            mine = self.held(s, h)
+            if hop < goal:
+
+                @pl.when(my_z == hop)
+                def _():
+                    self.up(s, h).wait_recv()
+                    mine[...] = mine[...] + from_low[self.w, s, h]
+                    self.up(s, h).start()
+
+            if NZ - 1 - hop > goal:
+
+                @pl.when(my_z == NZ - 1 - hop)
+                def _():
+                    self.down(s, h).wait_recv()
+                    mine[...] = mine[...] + from_high[self.w, s, h]
+                    self.down(s, h).start()
+
+        def step(self, t):
+            own, came = self.x, 1 - self.x
+            parts = [
+                (3, lambda s: self.relay(s, 2, came)),
+                (2, lambda s: self.relay(s, 2, own)),
+                (2, lambda s: self.relay(s, 1, came)),
+                (1, lambda s: self.relay(s, 1, own)),
+                (1, lambda s: self.from_ends(s, came)),
+                (0, self.add_y),
+                (0, lambda s: self.from_ends(s, own)),
+            ]
+            for lag, part in parts:
+                s = t - lag
+                if isinstance(t, int):
+                    if 0 <= s < PIECES:
+                        part(s)
+                else:
+                    pl.when((s >= 0) & (s < PIECES))(functools.partial(part, s))
 
         def collect(self, s):
             for h in range(2):
@@ -755,19 +773,12 @@
                     pl.when(my_z < goal)(self.up(s, h).wait_send)
                     pl.when(my_z > goal)(self.down(s, h).wait_send)
 
-    def rest_of_scatter(one, zero):
-        pl.loop(0, PIECES)(one.add_y)
-        pl.loop(0, PIECES)(one.from_ends)
-
-        def step(s, when):
-            when(s < PIECES, lambda: zero.add_y(s))
-            when(s < PIECES, lambda: one.relay(s, 1))
-            when((s > 0) & (s <= PIECES), lambda: one.relay(s - 1, 2))
-            when((s > 0) & (s <= PIECES), lambda: zero.from_ends(s - 1))
-            when((s > 1) & (s <= PIECES + 1), lambda: zero.relay(s - 2, 1))
-            when((s > 2) & (s <= PIECES + 2), lambda: zero.relay(s - 3, 2))
-
-        pl.loop(0, PIECES + 3)(lambda s: step(s, lambda is_so, do: pl.when(is_so)(do)))
+    def rest_of_scatter(one, zero, begun):
+        @pl.loop(begun, 2 * PIECES + 3)
+        def _(t):
+            one.step(t)
+            zero.step(t - PIECES)
+
         pl.loop(0, PIECES)(one.collect)
         pl.loop(0, PIECES)(zero.collect)
         one.sent()
@@ -784,11 +795,10 @@
             begin = jnp.where(seg == i, int(a), begin)
             end = jnp.where(seg == i, int(b), end)
         row = (me * 2 + role) * SHARD + lax.broadcasted_iota(jnp.int32, (SEGS, total.shape[0]), 1)
-        member = jnp.where((row >= begin) & (row < end), 1.0, 0.0)
-        squares = lax.dot_general(
-            member, total[...] * total[...], (((1,), (0,)), ((), ())),
-            precision=lax.Precision.HIGHEST, preferred_element_type=F32,
-        )
+        member = jnp.where((row >= begin) & (row < end), 1.0, 0.0).astype(BF)
+        square = total[...] * total[...]
+        high = square.astype(BF)
+        squares = mm(member, high) + mm(member, (square - high.astype(F32)).astype(BF))
         mine = jnp.broadcast_to(jnp.sum(squares, axis=1, keepdims=True), (SEGS, 128))
         for i, peer in enumerate((core_peer, y_peer, x_peer)):
             sq[2 * i] = mine
@@ -852,7 +862,7 @@
 
         copies["meta"].wait_recv()
 
-        @pl.loop(0, 12, unroll=4)
+        @pl.loop(0, 12, unroll=6)
         def _(i):
             c, p = i // 6, i % 6
             rows = pl.ds(al(c, TOK), TOK)
@@ -890,7 +900,7 @@
             count = jnp.where(col < PATCH, c0, jnp.where(col < PATCH_SLOT, 0.0, c1))
             count = jnp.where(col < PATCH_SLOT + PATCH, count, 0.0)
 
-            @pl.loop(0, 6, unroll=3)
+            @pl.loop(0, 6, unroll=6)
             def _(p):
                 qq = halves(q2[rows, pl.ds(al(p, 128), 128)]) * BF(0.125)
                 s = mm_nt(qq, kv[:, pl.ds(al(p, 128), 128)])
@@ -946,7 +956,7 @@
             rows = pl.ds(c * TOK, TOK)
             dx2_copy(c).wait_recv()
             t1[rows, :] = mm_nt(rb[rows, :], wide[:, UO_AT : UO_AT + D]).astype(BF)
-            pl.loop(0, 6, unroll=3)(functools.partial(attend_back, c, take_keys=take_keys))
+            pl.loop(0, 6, unroll=6)(functools.partial(attend_back, c, take_keys=take_keys))
 
         put_vector(at1[CROSS_OUT_BIAS], column_total(rb, slice(None)))
         matrix_grad(at1[CROSS_OUT], 6, a2T, rb)
@@ -984,7 +994,7 @@
         matrix_grad(at0[SELF_OUT], 6, amT, e1)
         t1[...] = mm_nt(e1[...], wide[:, WO_AT : WO_AT + D]).astype(BF)
 
-        @pl.loop(0, 12, unroll=4)
+        @pl.loop(0, 12, unroll=6)
         def _(i):
             c, p = i // 6, i % 6
             rows = pl.ds(al(c, TOK), TOK)
@@ -1000,6 +1010,7 @@
             big2[rows, klanes] = mm_tn(ds, qq).astype(BF)
             big2[rows, vlanes] = mm_tn(prob, do).astype(BF)
 
+        one.step(0)
         acc[...] = mm_nt(big2[:, : 3 * D], wide[:, : 3 * D])
 
         def write_dx0(rows, dv):
@@ -1011,6 +1022,7 @@
         dcap[...] = dx[first, :]
         dcap_b[...] = dx[later, :].astype(BF)
         copies["dcap"].start()
+        one.step(1)
         put_vector(at0[SELF_QUERY_BIAS], column_total(big2, slice(0, D)))
         put_vector(at0[SELF_VALUE_BIAS], column_total(big2, slice(2 * D, 3 * D)))
         matrix_grad(at0[SELF_QKV], 18, h1T, big2)
@@ -1020,7 +1032,7 @@
         pl.semaphore_wait(free, 1)
         zero.cast(CARRY)
         zero.add_core()
-        rest_of_scatter(one, zero)
+        rest_of_scatter(one, zero, 2)
         copies["out"].wait_recv()
         out[...] = ob[...]
         for name in ("dy", "dcap", "dtile"):
@@ -1134,7 +1146,7 @@
         pl.semaphore_wait(free, 1)
         zero.cast(CARRY)
         zero.add_core()
-        rest_of_scatter(one, zero)
+        rest_of_scatter(one, zero, 0)
         copies["dtile"].wait_recv()
         dtile[...] = dtile_b[0:PATCH, :].astype(F32)
         copies["dcap"].wait_recv()

time: 157 us -> 147 us (0.936)
  Pallas kernels: 143 us -> 132 us
    pallas_call x1, Pallas kernels: 143 us -> 132 us  [pair_call(): pl.pallas_call(pair_kernel, in_specs=[vm, vm, vm, sm, sm, sm, hbm], out_s...]
where the time goes in v3:
time: 147 us; the launch traced here: 146 us
  Pallas kernels  132 us (90%)
  other arithmetic  6.73 us (5%)
  local copies, waits for them, and re-layouts  3.9 us (3%)
  between operations  3.26 us (2%)
    pallas_call x1, Pallas kernels, pair_call(): pl.pallas_call(pair_kernel, in_specs=[vm, vm, vm, sm, sm, sm, hbm], out_s...  132 us
    mul x1, other arithmetic, adam_step(): -LEARN_RATE  4.54 us
    unnamed x14, local copies, waits for them, and re-layouts  3.9 us

profile of v3, /device:TPU:0, one launch (start us, length us, event | category | flops | bytes accessed | tf_op | source)
XLA Modules:
  0.0 146.2 jit_solution(4708311956993416618)
XLA Ops:
  0.7 0.8 and_reduce_fusion
  2.2 0.0 copy-start.4
  2.2 132.4 %shard_map.196 = (f32[2312,128]{1,0:T(8,128)}, f32[24,128]{1,0:T(8,128)}, bf16[2320,128]{1,0:T(8,128)(2,1)}, bf16[128,768]{1,0:T(8,128)(2,1)}, f32[128,768]{1,0:T(8,128)}, /*index=5*/f32[196,768]{1,0:T(8,128)}) custom-call(bf16[128,768]{1,0:T(8,128)(2,1)} %bitcast.10, bf16[196,768]{1,0:T(8,128)(2,1)} %bitcast.8, bf16[128,768]{1,0:T(8,128)(2,1)} %bitcast.11, ...), custom_call_target="tpu_custom_call" | custom-call | tf_op jit(solution)/shard_map/pallas_call | solution.py:1178
  134.6 0.0 copy-done.4
  134.6 1.3 sqrt_reduce_fusion
  136.6 0.0 copy-start.1
  136.7 4.5 %add_multiply_fusion = (f32[2312,128]{1,0:T(8,128)}, f32[2312,128]{1,0:T(8,128)}, f32[2312,128]{1,0:T(8,128)}) fusion(bf16[2320,128]{1,0:T(8,128)(2,1)} %get-tuple-element.20, s32[]{:T(128)S(6)} %select_n.33, bf16[36992,128]{1,0:T(8,128)(2,1)} %weights.1, s32[]{:T(128)S(6)} %select_n.32, pred[2312]{0:T(1024)(128)(4,1)S(1)} %and_reduce_fusion, pred[]{:T(512)S(6)} %eq.5, ...), kind=kLoop, calls=%fused_computation.2 | loop fusion | flops 5326848 | bytes 8288533 | tf_op jit(solution)/shard_map/mul | solution.py:195
  141.2 0.0 copy-start.3
  141.2 0.0 copy-start.2
  141.2 0.0 copy-done.1
  141.2 0.0 copy-start
  141.2 1.4 copy.24
  142.7 0.0 copy-done.3
  142.7 0.7 copy.29
  143.4 0.0 copy-done.2
  143.4 0.7 copy.30
  144.1 0.0 copy-done
  144.1 1.0 copy.31
  (1 shorter events, 0.0 us)
Async XLA Ops:
  2.2 132.4 %copy-start.4 = (f32[21,1]{1,0:T(8,128)S(1)}, f32[21,1]{1,0:T(8,128)}, u32[]{:S(2)}) copy-start(f32[21,1]{1,0:T(8,128)} %constant.96) | copy-start | bytes 256
  136.6 4.6 %copy-start.1 = (f32[196,768]{1,0:T(8,128)S(1)}, f32[196,768]{1,0:T(8,128)}, u32[]{:S(2)}) copy-start(f32[196,768]{1,0:T(8,128)} %get-tuple-element.17) | copy-start | bytes 1806340
  141.2 1.5 %copy-start.3 = (bf16[128,768]{1,0:T(8,128)(2,1)S(1)}, bf16[128,768]{1,0:T(8,128)(2,1)}, u32[]{:S(2)}) copy-start(bf16[128,768]{1,0:T(8,128)(2,1)} %get-tuple-element.15) | copy-start | bytes 589828
  141.2 2.1 %copy-start.2 = (f32[128,768]{1,0:T(8,128)S(1)}, f32[128,768]{1,0:T(8,128)}, u32[]{:S(2)}) copy-start(f32[128,768]{1,0:T(8,128)} %get-tuple-element.16) | copy-start | bytes 1179652
  141.2 2.9 %copy-start = (f32[2312,128]{1,0:T(8,128)S(1)}, f32[2312,128]{1,0:T(8,128)}, u32[]{:S(2)}) copy-start(f32[2312,128]{1,0:T(8,128)} %get-tuple-element.65) | copy-start | bytes 3551236

commit v4 on v3

--- a/solution.py
+++ b/solution.py
@@ -786,7 +786,7 @@
 
     def square_sums():
         total[SHARD:, :] = jnp.zeros((total.shape[0] - SHARD, 128), F32)
-        done = pltpu.make_async_copy(total.at[pl.ds(0, SHARD)], g_out, gsem)
+        done = pltpu.make_async_copy(total.at[pl.ds(0, OLD)], g_out, gsem)
         done.start()
         seg = lax.broadcasted_iota(jnp.int32, (SEGS, 1), 0)
         begin = jnp.full((SEGS, 1), 1 << 30, jnp.int32)
@@ -974,7 +974,7 @@
         def tile_grad(rows):
             return mm_nt(kv[rows, :], wide[:, UKV_AT : UKV_AT + 2 * D])
 
-        dtile[...] = tile_grad(pl.ds(0, PATCH_SENT))[:PATCH]
+        dtile[:, 0, :] = tile_grad(pl.ds(0, PATCH_SENT))[:PATCH]
         dtile_b[...] = tile_grad(pl.ds(PATCH_SLOT, PATCH_SENT)).astype(BF)
         copies["dtile"].start()
         one.add_core()
@@ -1031,8 +1031,9 @@
         ]
         pl.semaphore_wait(free, 1)
         zero.cast(CARRY)
+        one.step(2)
         zero.add_core()
-        rest_of_scatter(one, zero, 2)
+        rest_of_scatter(one, zero, 3)
         copies["out"].wait_recv()
         out[...] = ob[...]
         for name in ("dy", "dcap", "dtile"):
@@ -1148,7 +1149,7 @@
         zero.add_core()
         rest_of_scatter(one, zero, 0)
         copies["dtile"].wait_recv()
-        dtile[...] = dtile_b[0:PATCH, :].astype(F32)
+        dtile[:, 0, :] = dtile_b[0:PATCH, :].astype(F32)
         copies["dcap"].wait_recv()
         dcap[...] = dcap_b[...].astype(F32)
         for name in ("tile", "meta", "pfx", "out"):
@@ -1180,12 +1181,12 @@
         in_specs=[vm, vm, vm, sm, sm, sm, hbm],
         out_specs=[hbm, vm, hbm, vm, vm, vm],
         out_shape=[
-            S((SHARD, 128), F32),
+            S((OLD, 128), F32),
             S((SEGS, 128), F32),
             S((OLD, 128), BF),
             S((TOK, D), BF),
             S((TOK, D), F32),
-            S((PATCH, D), F32),
+            S((PATCH, 1, D), F32),
         ],
         scratch_shapes=[
             bf(16 * PADDED, 128), bf(D, WIDE), fl(CARRY + 7 * SHARD + PADDED, 128), bf(12 * both, KEYS),
@@ -1208,32 +1209,41 @@
     )(cap, tiles, d_out, index, valid, length, weights)
 
 
-def finish(shard_grad, old_weights, first_moment, second_moment, square_sums):
-    shard_rows = shard_grad.shape[0]
-    begin_row = lax.axis_index(BOTH) * shard_rows
+def pair_update(grads, old_weights, first_moment, second_moment, square_sums):
     seg_starts, seg_ends, decay_flags, seg_entries = segment_table(D, FF)
-    row_ids = begin_row + jnp.arange(shard_rows)
-    member = (row_ids[:, None] >= seg_starts[None, :]) & (row_ids[:, None] < seg_ends[None, :])
-    return adam_step(
-        shard_grad, member, decay_flags, old_weights, first_moment, second_moment, square_sums, seg_entries
-    )
+    grad_norm = jnp.sqrt(jnp.sum(square_sums))
+    tensor_rms = jnp.sqrt(square_sums / jnp.asarray(seg_entries, dtype=square_sums.dtype))
+    clipped = grads * jnp.minimum(1.0, CLIP_NORM / (grad_norm + 1e-06))
+    new_first = BETA_ONE * first_moment + (1.0 - BETA_ONE) * clipped
+    new_second = BETA_TWO * second_moment + (1.0 - BETA_TWO) * clipped * clipped
+    first_hat = new_first / (1.0 - BETA_ONE**STEP)
+    second_hat = new_second / (1.0 - BETA_TWO**STEP)
+    row = lax.axis_index(BOTH) * SHARD + lax.broadcasted_iota(jnp.int32, grads.shape, 0)
+    decays = row < 0
+    for start, end, decay in zip(seg_starts, seg_ends, decay_flags):
+        if decay:
+            decays = decays | ((row >= int(start)) & (row < int(end)))
+    decayed = jnp.where(decays, old_weights, 0.0)
+    update = -LEARN_RATE * (first_hat / (jnp.sqrt(second_hat) + ADAM_EPS) + DECAY_RATE * decayed)
+    return (update, new_first, new_second, grad_norm, tensor_rms)
 
 
 def pair_body(
     captions, tiles, tile_index, tile_valid, caption_len, weights, first_moment, second_moment, d_out
 ):
     me, f = lax.axis_index(DP), lax.axis_index(FSDP)
-    shard_grad, sums, old, out, caption_grad, tiles_grad = pair_call(
+    padded, sums, old, out, caption_grad, tiles_grad = pair_call(
         captions[0], tiles[0], d_out[0], tile_index, tile_valid, caption_len, weights
     )
+    shard_grad = padded[:SHARD]
     own = lax.dynamic_slice_in_dim(weights, ((2 * me + f) % 16) * SHARD, SHARD, 0)
     old = lax.dynamic_slice_in_dim(old, 8 * f, SHARD, 0)
     old_weights = jnp.where(me // 8 == f, own, old).astype(jnp.float32)
-    update, new_first, new_second, grad_norm, tensor_rms = finish(
+    update, new_first, new_second, grad_norm, tensor_rms = pair_update(
         shard_grad, old_weights, first_moment, second_moment, sums[:21, 0]
     )
     return (
-        out[None], caption_grad[None], tiles_grad[None], shard_grad, update, new_first, new_second,
+        out[None], caption_grad[None], jnp.swapaxes(tiles_grad, 0, 1), shard_grad, update, new_first, new_second,
         grad_norm, tensor_rms,
     )
 

time: 147 us -> 144 us (0.980)
  local copies, waits for them, and re-layouts: 3.9 us -> 2.26 us
    unnamed x14 -> x11, local copies, waits for them, and re-layouts: 3.9 us -> 2.26 us
where the time goes in v4:
time: 144 us
  Pallas kernels  132 us (92%)
  other arithmetic  6.23 us (4%)
  between operations  3.24 us (2%)
  local copies, waits for them, and re-layouts  2.26 us (2%)
    pallas_call x1, Pallas kernels, pair_call(): pl.pallas_call(pair_kernel, in_specs=[vm, vm, vm, sm, sm, sm, hbm], out_s...  132 us
    mul x1, other arithmetic, pair_update(): -LEARN_RATE  4.85 us

profile of v4, /device:TPU:0, one launch (start us, length us, event | category | flops | bytes accessed | tf_op | source)
XLA Modules:
  0.0 143.9 jit_solution(15507244077848576516)
XLA Ops:
  1.4 0.0 copy-start.3
  1.4 132.2 %shard_map.169 = (f32[2320,128]{1,0:T(8,128)}, f32[24,128]{1,0:T(8,128)}, bf16[2320,128]{1,0:T(8,128)(2,1)}, bf16[128,768]{1,0:T(8,128)(2,1)}, f32[128,768]{1,0:T(8,128)}, /*index=5*/f32[196,1,768]{2,1,0:T(1,128)}) custom-call(bf16[128,768]{1,0:T(8,128)(2,1)} %bitcast.10, bf16[196,768]{1,0:T(8,128)(2,1)} %bitcast.8, bf16[128,768]{1,0:T(8,128)(2,1)} %bitcast.11, ...), custom_call_target="tpu_custom_call" | custom-call | tf_op jit(solution)/shard_map/pallas_call | solution.py:1179
  133.6 0.0 copy-done.3
  133.6 1.3 sqrt_reduce_fusion
  135.6 0.0 copy-start.2
  135.7 0.0 copy-start.1
  135.7 4.8 %add_multiply_fusion = (f32[2312,128]{1,0:T(8,128)}, f32[2312,128]{1,0:T(8,128)}, f32[2312,128]{1,0:T(8,128)}, f32[2312,128]{1,0:T(8,128)}) fusion(bf16[2320,128]{1,0:T(8,128)(2,1)} %get-tuple-element.20, s32[]{:T(128)S(6)} %select_n.33, bf16[36992,128]{1,0:T(8,128)(2,1)} %weights.1, s32[]{:T(128)S(6)} %select_n.32, pred[2312]{0:T(1024)(128)(4,1)S(1)} %fusion.26, ...), kind=kLoop, calls=%fused_computation.2 | loop fusion | flops 5326848 | bytes 9472277 | tf_op jit(solution)/shard_map/mul | solution.py:1227
  140.5 0.0 copy-start
  140.5 0.0 copy-done.2
  140.5 0.7 copy.23
  141.2 0.0 copy-done.1
  141.2 0.7 copy.24
  141.9 0.0 copy-done
  142.0 0.8 copy.25
  (1 shorter events, 0.0 us)
Async XLA Ops:
  1.4 132.2 %copy-start.3 = (f32[21,1]{1,0:T(8,128)S(1)}, f32[21,1]{1,0:T(8,128)}, u32[]{:S(2)}) copy-start(f32[21,1]{1,0:T(8,128)} %constant.111) | copy-start | bytes 256
  135.6 4.9 %copy-start.2 = (bf16[128,768]{1,0:T(8,128)(2,1)S(1)}, bf16[128,768]{1,0:T(8,128)(2,1)}, u32[]{:S(2)}) copy-start(bf16[128,768]{1,0:T(8,128)(2,1)} %get-tuple-element.15) | copy-start | bytes 589828
  135.7 5.5 %copy-start.1 = (f32[128,768]{1,0:T(8,128)S(1)}, f32[128,768]{1,0:T(8,128)}, u32[]{:S(2)}) copy-start(f32[128,768]{1,0:T(8,128)} %get-tuple-element.16) | copy-start | bytes 1179652
  140.5 1.4 copy-start

commit v5 on v4

--- a/solution.py
+++ b/solution.py
@@ -520,7 +520,12 @@
     up_peer = at_dp(jnp.minimum(my_z + 1, NZ - 1), my_y, my_core)
     down_peer = at_dp(jnp.maximum(my_z - 1, 0), my_y, my_core)
     barrier = pltpu.get_barrier_semaphore()
-    for peer in (core_peer, y_peer, x_peer):
+    cube = []
+    for k in range(1, 8):
+        core = 1 - my_core if k & 1 else my_core
+        y = 1 - my_y if k & 2 else my_y
+        cube.append({DP: my_z * 4 + y * 2 + core, FSDP: other if k & 4 else role})
+    for peer in cube:
         pl.semaphore_signal(barrier, inc=1, device_id=peer, device_id_type=MESH)
     for step in range(1, NZ):
         peer = at_dp((my_z + step) % NZ, my_y, my_core)
@@ -588,7 +593,7 @@
     ).astype(F32)
 
     def all_here():
-        pl.semaphore_wait(barrier, 3 + NZ - 1)
+        pl.semaphore_wait(barrier, len(cube) + NZ - 1)
 
     def vector(row, at, n, col=0):
         block = fw[pl.ds(at, n // 128), :].astype(F32)
@@ -800,17 +805,22 @@
         high = square.astype(BF)
         squares = mm(member, high) + mm(member, (square - high.astype(F32)).astype(BF))
         mine = jnp.broadcast_to(jnp.sum(squares, axis=1, keepdims=True), (SEGS, 128))
-        for i, peer in enumerate((core_peer, y_peer, x_peer)):
-            sq[2 * i] = mine
-            swap = copy_to(peer, sq.at[2 * i], sq.at[2 * i + 1], sum_s.at[i], sum_r.at[i])
-            swap.start()
-            swap.wait()
-            mine = mine + sq[2 * i + 1]
-        sq[6] = mine
+        sq[0] = mine
+        swaps = [copy_to(p, sq.at[0], sq.at[k], sum_s.at[k], sum_r.at[k]) for k, p in enumerate(cube, 1)]
+        for c in swaps:
+            c.start()
+        for c in swaps:
+            c.wait()
+        mine = jnp.zeros((SEGS, 128), F32)
+        for k in range(8):
+            core = 1 - my_core if k & 1 else my_core
+            y = 1 - my_y if k & 2 else my_y
+            mine = mine + sq[core + 2 * y + 4 * (1 - role if k & 4 else role)]
+        sq[8] = mine
         sends = []
         for step in range(1, NZ):
             to = at_dp((my_z + step) % NZ, my_y, my_core)
-            sends.append(copy_to(to, sq.at[6], sq.at[6 + step], sum_s.at[2 + step], sum_r.at[2 + step]))
+            sends.append(copy_to(to, sq.at[8], sq.at[8 + step], sum_s.at[7 + step], sum_r.at[7 + step]))
             sends[-1].start()
         for c in sends:
             c.wait()
@@ -818,7 +828,7 @@
         for z in range(NZ):
             part = mine
             for step in range(1, NZ):
-                part = jnp.where((my_z - step + NZ) % NZ == z, sq[6 + step], part)
+                part = jnp.where((my_z - step + NZ) % NZ == z, sq[8 + step], part)
             whole = whole + part
         sums_out[...] = whole
         done.wait()
@@ -1197,11 +1207,11 @@
             fl(16, FF), fl(2, 8, 128), bf(TOK, D), fl(LEAD, 128), fl(LEAD, 128), fl(CARRY, 128),
             bf(TOK, D), bf(PATCH_SENT, D),
             bf(PIECES, 4 * PIECE, 128), bf(2, PIECES, 2 * PIECE, 128), bf(2, PIECES, PIECE, 128),
-            bf(2, PIECES, 2, PIECE, 128), bf(2, PIECES, 2, PIECE, 128), fl(2432, 128), fl(10, SEGS, 128),
+            bf(2, PIECES, 2, PIECE, 128), bf(2, PIECES, 2, PIECE, 128), fl(2432, 128), fl(8 + NZ, SEGS, 128),
             dma((5,)), dma, dma((16,)), dma((16,)),
             *[dma((2, PIECES)) for _ in range(6)],
             *[dma((2, PIECES, 2)) for _ in range(4)],
-            pltpu.SemaphoreType.REGULAR, dma((6,)), dma((6,)),
+            pltpu.SemaphoreType.REGULAR, dma((7 + NZ,)), dma((7 + NZ,)),
         ],
         compiler_params=pltpu.CompilerParams(
             collective_id=0, has_side_effects=True, vmem_limit_bytes=63 * 2**20

time: 144 us -> 142 us (0.986)
  Pallas kernels: 132 us -> 130 us
    pallas_call x1, Pallas kernels: 132 us -> 130 us  [pair_call(): pl.pallas_call(pair_kernel, in_specs=[vm, vm, vm, sm, sm, sm, hbm], out_s...]
where the time goes in v5:
time: 142 us
  Pallas kernels  130 us (92%)
  other arithmetic  6.23 us (4%)
  between operations  3.24 us (2%)
  local copies, waits for them, and re-layouts  2.26 us (2%)
    pallas_call x1, Pallas kernels, pair_call(): pl.pallas_call(pair_kernel, in_specs=[vm, vm, vm, sm, sm, sm, hbm], out_s...  130 us
    mul x1, other arithmetic, pair_update(): -LEARN_RATE  4.85 us

profile of v5, /device:TPU:0, one launch (start us, length us, event | category | flops | bytes accessed | tf_op | source)
XLA Modules:
  0.0 141.9 jit_solution(16391295262226423780)
XLA Ops:
  1.4 0.0 copy-start.3
  1.4 130.2 %shard_map.169 = (f32[2320,128]{1,0:T(8,128)}, f32[24,128]{1,0:T(8,128)}, bf16[2320,128]{1,0:T(8,128)(2,1)}, bf16[128,768]{1,0:T(8,128)(2,1)}, f32[128,768]{1,0:T(8,128)}, /*index=5*/f32[196,1,768]{2,1,0:T(1,128)}) custom-call(bf16[128,768]{1,0:T(8,128)(2,1)} %bitcast.10, bf16[196,768]{1,0:T(8,128)(2,1)} %bitcast.8, bf16[128,768]{1,0:T(8,128)(2,1)} %bitcast.11, ...), custom_call_target="tpu_custom_call" | custom-call | tf_op jit(solution)/shard_map/pallas_call | solution.py:1189
  131.6 0.0 copy-done.3
  131.6 1.3 sqrt_reduce_fusion
  133.7 0.0 copy-start.2
  133.7 0.0 copy-start.1
  133.7 4.8 %add_multiply_fusion = (f32[2312,128]{1,0:T(8,128)}, f32[2312,128]{1,0:T(8,128)}, f32[2312,128]{1,0:T(8,128)}, f32[2312,128]{1,0:T(8,128)}) fusion(bf16[2320,128]{1,0:T(8,128)(2,1)} %get-tuple-element.20, s32[]{:T(128)S(6)} %select_n.33, bf16[36992,128]{1,0:T(8,128)(2,1)} %weights.1, s32[]{:T(128)S(6)} %select_n.32, pred[2312]{0:T(1024)(128)(4,1)S(1)} %fusion.26, ...), kind=kLoop, calls=%fused_computation.2 | loop fusion | flops 5326848 | bytes 9472277 | tf_op jit(solution)/shard_map/mul | solution.py:1237
  138.5 0.0 copy-start
  138.5 0.0 copy-done.2
  138.5 0.7 copy.23
  139.2 0.0 copy-done.1
  139.2 0.7 copy.24
  140.0 0.0 copy-done
  140.0 0.8 copy.25
  (1 shorter events, 0.0 us)
Async XLA Ops:
  1.4 130.2 %copy-start.3 = (f32[21,1]{1,0:T(8,128)S(1)}, f32[21,1]{1,0:T(8,128)}, u32[]{:S(2)}) copy-start(f32[21,1]{1,0:T(8,128)} %constant.111) | copy-start | bytes 256
  133.7 4.9 %copy-start.2 = (bf16[128,768]{1,0:T(8,128)(2,1)S(1)}, bf16[128,768]{1,0:T(8,128)(2,1)}, u32[]{:S(2)}) copy-start(bf16[128,768]{1,0:T(8,128)(2,1)} %get-tuple-element.15) | copy-start | bytes 589828
  133.7 5.5 %copy-start.1 = (f32[128,768]{1,0:T(8,128)S(1)}, f32[128,768]{1,0:T(8,128)}, u32[]{:S(2)}) copy-start(f32[128,768]{1,0:T(8,128)} %get-tuple-element.16) | copy-start | bytes 1179652
  138.5 1.4 %copy-start = (f32[196,1,768]{2,1,0:T(1,128)S(1)}, f32[196,1,768]{2,1,0:T(1,128)}, u32[]{:S(2)}) copy-start(f32[196,1,768]{2,1,0:T(1,128)} %get-tuple-element.17) | copy-start | bytes 1806340

commit v6 on v5

--- a/solution.py
+++ b/solution.py
@@ -981,14 +981,15 @@
         one.cast(CARRY)
         carry[...] = gf[0:CARRY, :]
 
+        one.add_core()
+        pl.semaphore_signal(free, inc=1, device_id=core_peer, device_id_type=MESH)
+
         def tile_grad(rows):
             return mm_nt(kv[rows, :], wide[:, UKV_AT : UKV_AT + 2 * D])
 
         dtile[:, 0, :] = tile_grad(pl.ds(0, PATCH_SENT))[:PATCH]
         dtile_b[...] = tile_grad(pl.ds(PATCH_SLOT, PATCH_SENT)).astype(BF)
         copies["dtile"].start()
-        one.add_core()
-        pl.semaphore_signal(free, inc=1, device_id=core_peer, device_id_type=MESH)
         acc[...] = mm_nt(am[...], wide[:, UQ_AT : UQ_AT + D])
         e1 = h2
 

time: 142 us -> 143 us (level)
  no operation moved by 1% of the time
where the time goes in v6:
time: 143 us; the launch traced here: 142 us
  Pallas kernels  131 us (92%)
  other arithmetic  6.23 us (4%)
  between operations  3.24 us (2%)
  local copies, waits for them, and re-layouts  2.26 us (2%)
    pallas_call x1, Pallas kernels, pair_call(): pl.pallas_call(pair_kernel, in_specs=[vm, vm, vm, sm, sm, sm, hbm], out_s...  131 us
    mul x1, other arithmetic, pair_update(): -LEARN_RATE  4.85 us

profile of v6, /device:TPU:0, one launch (start us, length us, event | category | flops | bytes accessed | tf_op | source)
XLA Modules:
  0.0 142.5 jit_solution(4700574016146818208)
XLA Ops:
  1.4 0.0 copy-start.3
  1.4 130.8 %shard_map.169 = (f32[2320,128]{1,0:T(8,128)}, f32[24,128]{1,0:T(8,128)}, bf16[2320,128]{1,0:T(8,128)(2,1)}, bf16[128,768]{1,0:T(8,128)(2,1)}, f32[128,768]{1,0:T(8,128)}, /*index=5*/f32[196,1,768]{2,1,0:T(1,128)}) custom-call(bf16[128,768]{1,0:T(8,128)(2,1)} %bitcast.10, bf16[196,768]{1,0:T(8,128)(2,1)} %bitcast.8, bf16[128,768]{1,0:T(8,128)(2,1)} %bitcast.11, ...), custom_call_target="tpu_custom_call" | custom-call | tf_op jit(solution)/shard_map/pallas_call | solution.py:1190
  132.1 0.0 copy-done.3
  132.2 1.3 sqrt_reduce_fusion
  134.2 0.0 copy-start.2
  134.2 0.0 copy-start.1
  134.3 4.8 %add_multiply_fusion = (f32[2312,128]{1,0:T(8,128)}, f32[2312,128]{1,0:T(8,128)}, f32[2312,128]{1,0:T(8,128)}, f32[2312,128]{1,0:T(8,128)}) fusion(bf16[2320,128]{1,0:T(8,128)(2,1)} %get-tuple-element.20, s32[]{:T(128)S(6)} %select_n.33, bf16[36992,128]{1,0:T(8,128)(2,1)} %weights.1, s32[]{:T(128)S(6)} %select_n.32, pred[2312]{0:T(1024)(128)(4,1)S(1)} %fusion.26, ...), kind=kLoop, calls=%fused_computation.2 | loop fusion | flops 5326848 | bytes 9472277 | tf_op jit(solution)/shard_map/mul | solution.py:1238
  139.1 0.0 copy-start
  139.1 0.0 copy-done.2
  139.1 0.7 copy.23
  139.8 0.0 copy-done.1
  139.8 0.7 copy.24
  140.5 0.0 copy-done
  140.5 0.8 copy.25
  (1 shorter events, 0.0 us)
Async XLA Ops:
  1.4 130.8 %copy-start.3 = (f32[21,1]{1,0:T(8,128)S(1)}, f32[21,1]{1,0:T(8,128)}, u32[]{:S(2)}) copy-start(f32[21,1]{1,0:T(8,128)} %constant.111) | copy-start | bytes 256
  134.2 4.9 %copy-start.2 = (bf16[128,768]{1,0:T(8,128)(2,1)S(1)}, bf16[128,768]{1,0:T(8,128)(2,1)}, u32[]{:S(2)}) copy-start(bf16[128,768]{1,0:T(8,128)(2,1)} %get-tuple-element.15) | copy-start | bytes 589828
  134.2 5.5 %copy-start.1 = (f32[128,768]{1,0:T(8,128)S(1)}, f32[128,768]{1,0:T(8,128)}, u32[]{:S(2)}) copy-start(f32[128,768]{1,0:T(8,128)} %get-tuple-element.16) | copy-start | bytes 1179652
  139.1 1.4 %copy-start = (f32[196,1,768]{2,1,0:T(1,128)S(1)}, f32[196,1,768]{2,1,0:T(1,128)}, u32[]{:S(2)}) copy-start(f32[196,1,768]{2,1,0:T(1,128)} %get-tuple-element.17) | copy-start | bytes 1806340
